TPU v7x, 32 devices: a whole 2x2x4 slice. The times are simulated.
32 devices in a mesh: cfg: 2 (over core), section: 2 (over y), tp: 8 (over z, x).
Axes of the slice: x: 2, y: 2, z: 4, core: 2. Of those that a mesh axis runs over, the one named last changes fastest.
Arguments:
- latent: bfloat16 [512, 6144], replicated, may hold values from -6 to 6
- condition: bfloat16 [2, 6144], P('cfg'), may hold values from -3 to 3
- gain: bfloat16 [2, 6144], P('section'), may hold values from 0.099609375 to 1.8984375
- w_query: bfloat16 [2, 6144, 1024], P('section', None, 'tp'), may hold values from -0.078125 to 0.078125
- w_key: bfloat16 [2, 6144, 1024], P('section', None, 'tp'), may hold values from -0.078125 to 0.078125
- w_value: bfloat16 [2, 6144, 1024], P('section', None, 'tp'), may hold values from -0.078125 to 0.078125
- w_out: bfloat16 [2, 1024, 6144], P('section', 'tp'), may hold values from -0.5 to 0.5
- stale_keys: bfloat16 [2, 2, 512, 1024], P('cfg', 'section', None, 'tp'), may hold values from -150 to 150
- stale_values: bfloat16 [2, 2, 512, 1024], P('cfg', 'section', None, 'tp'), may hold values from -6 to 6
- patch_order: int32 [4], replicated, may hold values from 0 to 3, each once
- stale_mask: int32 [4], replicated, may hold values 0 or 1
Outputs:
- guided: bfloat16 [512, 6144], P(('cfg', 'section'), 'tp')
- new_keys: bfloat16 [2, 2, 512, 1024], P('cfg', 'section', None, 'tp')
- new_values: bfloat16 [2, 2, 512, 1024], P('cfg', 'section', None, 'tp')
Inputs may be any that keep to these rules, and one draw needn't show every extreme that they name: `patch_order`: each of the 4 patch numbers exactly once.
All inputs are finite; a program needn't handle non-finite values.
Results may differ from a plain program's by a relative error of at most 0.035.
Values may be sent and summed in bfloat16 or wider, within the bound.
A program may use at most 64 MiB of HBM per device.

v0:
```python
import jax
import jax.numpy as jnp
from jax import lax
from jax.sharding import PartitionSpec as P

HEAD_DIM = 128
PATCH_LEN = 128
PATCHES = 4


GUIDE_SCALE = 3.0
NORM_EPS = 1e-06


def passed_along(block, axis, distance):
    devices = range(lax.axis_size(axis))
    route = [((i - distance) % len(devices), i) for i in devices]
    return lax.ppermute(block, axis, route)


def partner_2(x, axis, stride):
    return lax.ppermute(x, axis, [(i, i ^ 1 << stride) for i in range(lax.axis_size(axis))])


def attend_rows(query, fresh_keys, fresh_values, old_keys, old_values, fresh_open, stale_open):
    row_count = query.shape[0]
    head_count = query.shape[1] // HEAD_DIM
    key_count = fresh_keys.shape[0]
    factor = HEAD_DIM ** (-0.5)
    query_heads = query.reshape(row_count, head_count, HEAD_DIM)

    def split(array):
        return array.reshape(key_count, head_count, HEAD_DIM)

    fresh_scores = (
        jnp.einsum(
            "rhe,she->hrs", query_heads, split(fresh_keys), preferred_element_type=jnp.float32
        )
        * factor
    )
    old_scores = (
        jnp.einsum("rhe,she->hrs", query_heads, split(old_keys), preferred_element_type=jnp.float32)
        * factor
    )
    fresh_scores = jnp.where(fresh_open[None], fresh_scores, -jnp.inf)
    old_scores = jnp.where(stale_open[None], old_scores, -jnp.inf)
    top = jnp.maximum(
        jnp.max(fresh_scores, axis=2, keepdims=True), jnp.max(old_scores, axis=2, keepdims=True)
    )
    fresh_exp = jnp.exp(fresh_scores - top)
    old_exp = jnp.exp(old_scores - top)
    total = jnp.sum(fresh_exp, axis=2, keepdims=True) + jnp.sum(old_exp, axis=2, keepdims=True)
    fresh_weight = (fresh_exp / total).astype(jnp.bfloat16)
    old_weight = (old_exp / total).astype(jnp.bfloat16)
    mixed = jnp.einsum(
        "hrs,she->rhe", fresh_weight, split(fresh_values), preferred_element_type=jnp.float32
    )
    mixed = mixed + jnp.einsum(
        "hrs,she->rhe", old_weight, split(old_values), preferred_element_type=jnp.float32
    )
    return mixed.reshape(row_count, head_count * HEAD_DIM).astype(jnp.bfloat16)


def body(
    latent,
    condition,
    gain,
    w_query,
    w_key,
    w_value,
    w_out,
    stale_keys,
    stale_values,
    patch_order,
    stale_mask,
):
    tp_count = lax.axis_size("tp")
    section_count = lax.axis_size("section")
    section = lax.axis_index("section")
    tp_index = lax.axis_index("tp")
    branch = lax.axis_index("cfg")
    width = latent.shape[1]
    local_width = width // tp_count
    seq_len = latent.shape[0]
    query_w = w_query[0]
    key_w = w_key[0]
    value_w = w_value[0]
    out_w = w_out[0]
    head_width = query_w.shape[1]
    gain_row = gain[0].astype(jnp.float32)
    old_keys = stale_keys[0, 0]
    old_values = stale_values[0, 0]
    numbers = jnp.arange(PATCHES, dtype=jnp.int32)
    placed = jnp.sum(
        numbers[:, None] * (patch_order[:, None] == numbers[None, :]).astype(jnp.int32), axis=0
    )
    key_pos = jnp.repeat(placed, PATCH_LEN)
    key_open = jnp.repeat(stale_mask, PATCH_LEN) == 1
    group = 1
    group_rows = group * PATCH_LEN
    slots = PATCHES // group
    ticks = slots + section_count - 1
    last_section = section_count - 1
    entry = (latent.astype(jnp.float32) + condition[0].astype(jnp.float32)[None, :]).astype(
        jnp.bfloat16
    )
    entry = lax.dynamic_slice_in_dim(entry, tp_index * local_width, local_width, 1)

    def advance(step_index, carry):
        incoming, fresh_keys, fresh_values, finished = carry
        slot = step_index - section
        live = (slot >= 0) & (slot < slots)
        slot = jnp.clip(slot, 0, slots - 1)
        members = [lax.dynamic_index_in_dim(patch_order, slot * group + 0, 0, keepdims=False)]
        first_rows = jnp.concatenate(
            [lax.dynamic_slice_in_dim(entry, patch * PATCH_LEN, PATCH_LEN, 0) for patch in members],
            axis=0,
        )
        current = jnp.where(section == 0, first_rows, incoming)
        full_rows = lax.all_gather(current, "tp", axis=1, tiled=True)
        row_float = full_rows.astype(jnp.float32)
        scaled = row_float * lax.rsqrt(
            jnp.mean(row_float * row_float, axis=1, keepdims=True) + NORM_EPS
        )
        normed = (scaled * gain_row[None, :]).astype(jnp.bfloat16)
        query = jnp.dot(normed, query_w, preferred_element_type=jnp.float32).astype(jnp.bfloat16)
        keys = jnp.dot(normed, key_w, preferred_element_type=jnp.float32).astype(jnp.bfloat16)
        values = jnp.dot(normed, value_w, preferred_element_type=jnp.float32).astype(jnp.bfloat16)
        member = 0
        patch = members[member]
        fresh_keys = jnp.where(
            live,
            lax.dynamic_update_slice_in_dim(fresh_keys, keys, patch * PATCH_LEN, 0),
            fresh_keys,
        )
        fresh_values = jnp.where(
            live,
            lax.dynamic_update_slice_in_dim(fresh_values, values, patch * PATCH_LEN, 0),
            fresh_values,
        )
        query_pos = slot * group + jnp.repeat(jnp.arange(group, dtype=jnp.int32), PATCH_LEN)
        fresh_open = key_pos[None, :] <= query_pos[:, None]
        stale_open = (key_pos[None, :] > query_pos[:, None]) & key_open[None, :]
        attention = attend_rows(
            query, fresh_keys, fresh_values, old_keys, old_values, fresh_open, stale_open
        )
        term = jnp.dot(attention, out_w, preferred_element_type=jnp.float32)
        summed = lax.psum_scatter(
            term.astype(jnp.bfloat16), "tp", scatter_dimension=1, tiled=True
        ).astype(jnp.float32)
        result = (current.astype(jnp.float32) + summed).astype(jnp.bfloat16)
        outgoing = passed_along(result, "section", 1)
        final_rows = jnp.where(section == last_section, result, outgoing)
        final_slot = step_index - last_section
        done = (final_slot >= 0) & (final_slot < slots)
        final_slot = jnp.clip(final_slot, 0, slots - 1)
        member = 0
        patch = lax.dynamic_index_in_dim(
            patch_order, final_slot * group + member, 0, keepdims=False
        )
        finished = jnp.where(
            done,
            lax.dynamic_update_slice_in_dim(finished, final_rows, patch * PATCH_LEN, 0),
            finished,
        )
        return (outgoing, fresh_keys, fresh_values, finished)

    start = (
        jnp.zeros((group_rows, local_width), jnp.bfloat16),
        jnp.zeros((seq_len, head_width), jnp.bfloat16),
        jnp.zeros((seq_len, head_width), jnp.bfloat16),
        jnp.zeros((seq_len, local_width), jnp.bfloat16),
    )
    incoming, fresh_keys, fresh_values, finished = lax.fori_loop(0, ticks, advance, start)
    quarter = seq_len // 4
    own_block = branch * 2 + section
    other_block = (1 - branch) * 2 + section
    outbound = lax.dynamic_slice_in_dim(finished, other_block * quarter, quarter, 0)
    own_rows = lax.dynamic_slice_in_dim(finished, own_block * quarter, quarter, 0)
    partner = partner_2(outbound, "cfg", 0)
    conditioned = jnp.where(branch == 0, own_rows, partner).astype(jnp.float32)
    unconditioned = jnp.where(branch == 0, partner, own_rows).astype(jnp.float32)
    guided = (unconditioned + GUIDE_SCALE * (conditioned - unconditioned)).astype(jnp.bfloat16)
    return (guided, fresh_keys[None, None], fresh_values[None, None])


def solution(mesh):
    placed = (
        P(),
        P("cfg", None),
        P("section", None),
        P("section", None, "tp"),
        P("section", None, "tp"),
        P("section", None, "tp"),
        P("section", "tp", None),
        P("cfg", "section", None, "tp"),
        P("cfg", "section", None, "tp"),
        P(),
        P(),
    )
    return jax.shard_map(
        body,
        mesh=mesh,
        in_specs=placed,
        out_specs=(
            P(("cfg", "section"), "tp"),
            P("cfg", "section", None, "tp"),
            P("cfg", "section", None, "tp"),
        ),
        check_vma=False,
    )
```

profile of v0, /device:TPU:0, one launch (start us, length us, event | category | flops | bytes accessed | tf_op | source)
XLA Modules:
  0.0 655.9 jit_solution(10256461932321346840)
XLA Ops:
  10.4 2.2 add_convert_fusion.1
  12.7 634.0 %while.22 = (s32[]{:T(128)}, bf16[128,768]{1,0:T(8,128)(2,1)S(1)}, bf16[512,128]{1,0:T(8,128)(2,1)S(1)}, bf16[512,128]{1,0:T(8,128)(2,1)S(1)}, bf16[512,768]{1,0...) while((s32[]{:T(128)}, bf16[128,768]{1,0:T(8,128)(2,1)S(1)}, ...), condition=%wide.region_8.9_spmd.clone, body=%wide.region_1.8_spmd.clone.sunk | while | flops 886849920 | bytes 49730792 | solution.py:174
  15.9 47.6 %all-gather.2.cloned.1.call-done = bf16[128,6144]{1,0:T(8,128)(2,1)} async-done(((bf16[128,768]{1,0:T(8,128)(2,1)}), bf16[128,6144]{1,0:T(8,128)(2,1)}) %all-gather.2.cloned.1.call-update) | async-done | bytes 1572880 | tf_op jit(solution)/shard_map/while/body/eval_jaxpr/all_gather | solution.py:120
  63.5 1.9 fusion.75
  65.5 2.2 convolution_convert_fusion.6
  70.3 2.0 convolution_convert_fusion.7
  72.4 63.4 %reduce-scatter.2.cloned.1.call-done = bf16[128,768]{1,0:T(8,128)(2,1)} async-done(((bf16[128,6144]{1,0:T(8,128)(2,1)}), bf16[128,768]{1,0:T(8,128)(2,1)}) %reduce-scatter.2.cloned.1.call-update) | async-done | bytes 196624 | tf_op jit(solution)/shard_map/while/body/eval_jaxpr/reduce_scatter | solution.py:148
  138.9 3.6 collective-permute-done
  145.8 43.8 %all-gather.2.cloned.1.call-done = bf16[128,6144]{1,0:T(8,128)(2,1)} async-done(((bf16[128,768]{1,0:T(8,128)(2,1)}), bf16[128,6144]{1,0:T(8,128)(2,1)}) %all-gather.2.cloned.1.call-update) | async-done | bytes 1572880 | tf_op jit(solution)/shard_map/while/body/eval_jaxpr/all_gather | solution.py:120
  189.6 1.9 fusion.75
  191.5 2.2 convolution_convert_fusion.6
  196.4 2.0 convolution_convert_fusion.7
  198.4 63.4 %reduce-scatter.2.cloned.1.call-done = bf16[128,768]{1,0:T(8,128)(2,1)} async-done(((bf16[128,6144]{1,0:T(8,128)(2,1)}), bf16[128,768]{1,0:T(8,128)(2,1)}) %reduce-scatter.2.cloned.1.call-update) | async-done | bytes 196624 | tf_op jit(solution)/shard_map/while/body/eval_jaxpr/reduce_scatter | solution.py:148
  264.9 3.6 collective-permute-done
  271.8 43.5 %all-gather.2.cloned.1.call-done = bf16[128,6144]{1,0:T(8,128)(2,1)} async-done(((bf16[128,768]{1,0:T(8,128)(2,1)}), bf16[128,6144]{1,0:T(8,128)(2,1)}) %all-gather.2.cloned.1.call-update) | async-done | bytes 1572880 | tf_op jit(solution)/shard_map/while/body/eval_jaxpr/all_gather | solution.py:120
  315.4 1.9 fusion.75
  317.3 2.2 convolution_convert_fusion.6
  322.1 2.0 convolution_convert_fusion.7
  324.2 63.4 %reduce-scatter.2.cloned.1.call-done = bf16[128,768]{1,0:T(8,128)(2,1)} async-done(((bf16[128,6144]{1,0:T(8,128)(2,1)}), bf16[128,768]{1,0:T(8,128)(2,1)}) %reduce-scatter.2.cloned.1.call-update) | async-done | bytes 196624 | tf_op jit(solution)/shard_map/while/body/eval_jaxpr/reduce_scatter | solution.py:148
  390.7 3.6 collective-permute-done
  397.6 43.8 %all-gather.2.cloned.1.call-done = bf16[128,6144]{1,0:T(8,128)(2,1)} async-done(((bf16[128,768]{1,0:T(8,128)(2,1)}), bf16[128,6144]{1,0:T(8,128)(2,1)}) %all-gather.2.cloned.1.call-update) | async-done | bytes 1572880 | tf_op jit(solution)/shard_map/while/body/eval_jaxpr/all_gather | solution.py:120
  441.4 1.9 fusion.75
  443.4 2.2 convolution_convert_fusion.6
  448.2 2.0 convolution_convert_fusion.7
  450.2 63.5 %reduce-scatter.2.cloned.1.call-done = bf16[128,768]{1,0:T(8,128)(2,1)} async-done(((bf16[128,6144]{1,0:T(8,128)(2,1)}), bf16[128,768]{1,0:T(8,128)(2,1)}) %reduce-scatter.2.cloned.1.call-update) | async-done | bytes 196624 | tf_op jit(solution)/shard_map/while/body/eval_jaxpr/reduce_scatter | solution.py:148
  516.8 3.6 collective-permute-done
  523.8 43.9 %all-gather.2.cloned.1.call-done = bf16[128,6144]{1,0:T(8,128)(2,1)} async-done(((bf16[128,768]{1,0:T(8,128)(2,1)}), bf16[128,6144]{1,0:T(8,128)(2,1)}) %all-gather.2.cloned.1.call-update) | async-done | bytes 1572880 | tf_op jit(solution)/shard_map/while/body/eval_jaxpr/all_gather | solution.py:120
  567.6 1.9 fusion.75
  569.5 2.2 convolution_convert_fusion.6
  574.4 2.0 convolution_convert_fusion.7
  576.4 63.5 %reduce-scatter.2.cloned.1.call-done = bf16[128,768]{1,0:T(8,128)(2,1)} async-done(((bf16[128,6144]{1,0:T(8,128)(2,1)}), bf16[128,768]{1,0:T(8,128)(2,1)}) %reduce-scatter.2.cloned.1.call-update) | async-done | bytes 196624 | tf_op jit(solution)/shard_map/while/body/eval_jaxpr/reduce_scatter | solution.py:148
  643.0 3.6 collective-permute-done
  (170 shorter events, 44.0 us)
Async XLA Ops:
  7.2 5.5 copy-start.7
  7.2 5.5 copy-start.5
  7.2 5.5 copy-start.4
  7.2 5.5 copy-start.2
  12.7 50.8 %all-gather.2.cloned.1.call-start = ((), (), s32[]{:S(2)}) async-start(), calls=%async_computation.1 | async-start | bytes 1769472 | tf_op jit(solution)/shard_map/while/body/eval_jaxpr/all_gather | solution.py:120
  15.7 120.0 %reduce-scatter.2.cloned.1.call-start = ((), (), s32[]{:S(2)}) async-start(), calls=%async_computation.2 | async-start | bytes 1769472 | tf_op jit(solution)/shard_map/while/body/eval_jaxpr/reduce_scatter | solution.py:148
  65.5 2.2 copy-start.9
  72.3 63.4 %copy-start = (bf16[128,768]{1,0:T(8,128)(2,1)S(1)}, bf16[128,768]{1,0:T(8,128)(2,1)}, u32[]{:S(2)}) copy-start(bf16[128,768]{1,0:T(8,128)(2,1)} %dynamic-slice_select_fusion.2) | copy-start | bytes 589828 | tf_op jit(solution)/shard_map/while
  136.7 5.7 collective-permute-start
  142.6 47.0 %all-gather.2.cloned.1.call-start = ((), (), s32[]{:S(2)}) async-start(), calls=%async_computation.1 | async-start | bytes 1769472 | tf_op jit(solution)/shard_map/while/body/eval_jaxpr/all_gather | solution.py:120
  145.6 116.2 %reduce-scatter.2.cloned.1.call-start = ((), (), s32[]{:S(2)}) async-start(), calls=%async_computation.2 | async-start | bytes 1769472 | tf_op jit(solution)/shard_map/while/body/eval_jaxpr/reduce_scatter | solution.py:148
  191.5 2.2 copy-start.9
  198.4 63.4 %copy-start = (bf16[128,768]{1,0:T(8,128)(2,1)S(1)}, bf16[128,768]{1,0:T(8,128)(2,1)}, u32[]{:S(2)}) copy-start(bf16[128,768]{1,0:T(8,128)(2,1)} %dynamic-slice_select_fusion.2) | copy-start | bytes 589828 | tf_op jit(solution)/shard_map/while
  262.8 5.7 collective-permute-start
  268.6 46.8 %all-gather.2.cloned.1.call-start = ((), (), s32[]{:S(2)}) async-start(), calls=%async_computation.1 | async-start | bytes 1769472 | tf_op jit(solution)/shard_map/while/body/eval_jaxpr/all_gather | solution.py:120
  271.6 116.0 %reduce-scatter.2.cloned.1.call-start = ((), (), s32[]{:S(2)}) async-start(), calls=%async_computation.2 | async-start | bytes 1769472 | tf_op jit(solution)/shard_map/while/body/eval_jaxpr/reduce_scatter | solution.py:148
  317.3 2.2 copy-start.9
  324.2 63.4 %copy-start = (bf16[128,768]{1,0:T(8,128)(2,1)S(1)}, bf16[128,768]{1,0:T(8,128)(2,1)}, u32[]{:S(2)}) copy-start(bf16[128,768]{1,0:T(8,128)(2,1)} %dynamic-slice_select_fusion.2) | copy-start | bytes 589828 | tf_op jit(solution)/shard_map/while
  388.6 5.7 collective-permute-start
  394.4 47.0 %all-gather.2.cloned.1.call-start = ((), (), s32[]{:S(2)}) async-start(), calls=%async_computation.1 | async-start | bytes 1769472 | tf_op jit(solution)/shard_map/while/body/eval_jaxpr/all_gather | solution.py:120
  397.4 116.4 %reduce-scatter.2.cloned.1.call-start = ((), (), s32[]{:S(2)}) async-start(), calls=%async_computation.2 | async-start | bytes 1769472 | tf_op jit(solution)/shard_map/while/body/eval_jaxpr/reduce_scatter | solution.py:148
  443.3 2.2 copy-start.9
  450.2 63.5 %copy-start = (bf16[128,768]{1,0:T(8,128)(2,1)S(1)}, bf16[128,768]{1,0:T(8,128)(2,1)}, u32[]{:S(2)}) copy-start(bf16[128,768]{1,0:T(8,128)(2,1)} %dynamic-slice_select_fusion.2) | copy-start | bytes 589828 | tf_op jit(solution)/shard_map/while
  514.7 5.7 collective-permute-start
  520.5 47.1 %all-gather.2.cloned.1.call-start = ((), (), s32[]{:S(2)}) async-start(), calls=%async_computation.1 | async-start | bytes 1769472 | tf_op jit(solution)/shard_map/while/body/eval_jaxpr/all_gather | solution.py:120
  523.5 116.4 %reduce-scatter.2.cloned.1.call-start = ((), (), s32[]{:S(2)}) async-start(), calls=%async_computation.2 | async-start | bytes 1769472 | tf_op jit(solution)/shard_map/while/body/eval_jaxpr/reduce_scatter | solution.py:148
  569.5 2.2 copy-start.9
  576.4 63.5 %copy-start = (bf16[128,768]{1,0:T(8,128)(2,1)S(1)}, bf16[128,768]{1,0:T(8,128)(2,1)}, u32[]{:S(2)}) copy-start(bf16[128,768]{1,0:T(8,128)(2,1)} %dynamic-slice_select_fusion.2) | copy-start | bytes 589828 | tf_op jit(solution)/shard_map/while
  640.9 5.7 collective-permute-start
  646.7 2.3 copy-start.3
  646.7 2.3 copy-start.6
  646.8 1.5 collective-permute-start.1
  (10 other events, 17.4 us)
Sparse Core Ops, SparseCore 0:
  16.3 47.1 all-gather.1
  72.5 63.2 reduce-scatter.1
  146.2 43.3 all-gather.1
  198.5 63.2 reduce-scatter.1
  271.9 43.3 all-gather.1
  324.3 63.2 reduce-scatter.1
  398.0 43.3 all-gather.1
  450.4 63.3 reduce-scatter.1
  524.2 43.4 all-gather.1
  576.6 63.2 reduce-scatter.1
where the time goes:
time: 656 us
  waiting for transfers between devices  559 us (85%)
  matrix products  32.8 us (5%)
  other arithmetic  30.7 us (5%)
  between operations  14.2 us (2%)
  starting transfers between devices  8.23 us (1%)
  loops' own time  6.95 us (1%)
    reduce_scatter x5, waiting for transfers between devices, advance(): lax.psum_scatter(term.astype(jnp.bfloat16), 'tp', scatter_dimension=1, ti...  317 us
    all_gather x5, waiting for transfers between devices, advance(): full_rows = lax.all_gather(current, 'tp', axis=1, tiled=True)  223 us
    ppermute x5, waiting for transfers between devices, passed_along(): return lax.ppermute(block, axis, route)  18 us
  transfers between devices with their start and end apart: 16, of which 16 were waited for; matrix products, arithmetic and copies ran while one was open for 0% of the time, Pallas kernels for 0%

commit v1 on v0

v1 whole, which is shorter than its diff:
```python
import jax
import jax.numpy as jnp
from jax import lax
from jax.sharding import PartitionSpec as P

HEAD_DIM = 128
PATCH_LEN = 128
PATCHES = 4


GUIDE_SCALE = 3.0
NORM_EPS = 1e-06


def passed_along(block, axis, distance):
    devices = range(lax.axis_size(axis))
    route = [((i - distance) % len(devices), i) for i in devices]
    return lax.ppermute(block, axis, route)


def partner_2(x, axis, stride):
    return lax.ppermute(x, axis, [(i, i ^ 1 << stride) for i in range(lax.axis_size(axis))])


def attend_rows(query, fresh_keys, fresh_values, old_keys, old_values, fresh_open, stale_open):
    row_count = query.shape[0]
    head_count = query.shape[1] // HEAD_DIM
    key_count = fresh_keys.shape[0]
    factor = HEAD_DIM ** (-0.5)
    query_heads = query.reshape(row_count, head_count, HEAD_DIM)

    def split(array):
        return array.reshape(key_count, head_count, HEAD_DIM)

    fresh_scores = (
        jnp.einsum(
            "rhe,she->hrs", query_heads, split(fresh_keys), preferred_element_type=jnp.float32
        )
        * factor
    )
    old_scores = (
        jnp.einsum("rhe,she->hrs", query_heads, split(old_keys), preferred_element_type=jnp.float32)
        * factor
    )
    fresh_scores = jnp.where(fresh_open[None], fresh_scores, -jnp.inf)
    old_scores = jnp.where(stale_open[None], old_scores, -jnp.inf)
    top = jnp.maximum(
        jnp.max(fresh_scores, axis=2, keepdims=True), jnp.max(old_scores, axis=2, keepdims=True)
    )
    fresh_exp = jnp.exp(fresh_scores - top)
    old_exp = jnp.exp(old_scores - top)
    total = jnp.sum(fresh_exp, axis=2, keepdims=True) + jnp.sum(old_exp, axis=2, keepdims=True)
    fresh_weight = (fresh_exp / total).astype(jnp.bfloat16)
    old_weight = (old_exp / total).astype(jnp.bfloat16)
    mixed = jnp.einsum(
        "hrs,she->rhe", fresh_weight, split(fresh_values), preferred_element_type=jnp.float32
    )
    mixed = mixed + jnp.einsum(
        "hrs,she->rhe", old_weight, split(old_values), preferred_element_type=jnp.float32
    )
    return mixed.reshape(row_count, head_count * HEAD_DIM).astype(jnp.bfloat16)


def body(
    latent,
    condition,
    gain,
    w_query,
    w_key,
    w_value,
    w_out,
    stale_keys,
    stale_values,
    patch_order,
    stale_mask,
):
    tp_count = lax.axis_size("tp")
    section_count = lax.axis_size("section")
    section = lax.axis_index("section")
    tp_index = lax.axis_index("tp")
    branch = lax.axis_index("cfg")
    width = latent.shape[1]
    local_width = width // tp_count
    seq_len = latent.shape[0]
    query_w = w_query[0]
    key_w = w_key[0]
    value_w = w_value[0]
    out_w = w_out[0]
    gain_row = gain[0].astype(jnp.float32)
    old_keys = stale_keys[0, 0]
    old_values = stale_values[0, 0]
    numbers = jnp.arange(PATCHES, dtype=jnp.int32)
    placed = jnp.sum(
        numbers[:, None] * (patch_order[:, None] == numbers[None, :]).astype(jnp.int32), axis=0
    )
    pos = jnp.repeat(placed, PATCH_LEN)
    key_open = jnp.repeat(stale_mask, PATCH_LEN) == 1
    fresh_open = pos[None, :] <= pos[:, None]
    stale_open = (pos[None, :] > pos[:, None]) & key_open[None, :]
    entry = (latent.astype(jnp.float32) + condition[0].astype(jnp.float32)[None, :]).astype(
        jnp.bfloat16
    )
    gather_weights = 2 * tp_count * out_w.shape[0] <= seq_len * 4
    if gather_weights:
        first_out = lax.all_gather(passed_along(out_w, "section", 1), "tp", axis=0, tiled=True)

    def project(rows):
        row_float = rows.astype(jnp.float32)
        scaled = row_float * lax.rsqrt(
            jnp.mean(row_float * row_float, axis=1, keepdims=True) + NORM_EPS
        )
        normed = (scaled * gain_row[None, :]).astype(jnp.bfloat16)
        return [
            jnp.dot(normed, w, preferred_element_type=jnp.float32).astype(jnp.bfloat16)
            for w in (query_w, key_w, value_w)
        ]

    query0, keys0, values0 = project(entry)
    mixed0 = attend_rows(query0, keys0, values0, old_keys, old_values, fresh_open, stale_open)
    if gather_weights:
        mixed0 = lax.all_gather(passed_along(mixed0, "section", 1), "tp", axis=1, tiled=True)
        summed = jnp.dot(mixed0, first_out, preferred_element_type=jnp.float32)
        second = (entry.astype(jnp.float32) + summed).astype(jnp.bfloat16)
    else:
        term = jnp.dot(mixed0, out_w, preferred_element_type=jnp.float32)
        summed = lax.psum_scatter(
            term.astype(jnp.bfloat16), "tp", scatter_dimension=1, tiled=True
        ).astype(jnp.float32)
        current = lax.dynamic_slice_in_dim(entry, tp_index * local_width, local_width, 1)
        second = (current.astype(jnp.float32) + summed).astype(jnp.bfloat16)
        second = lax.all_gather(passed_along(second, "section", 1), "tp", axis=1, tiled=True)
    query1, keys1, values1 = project(second)
    mixed1 = attend_rows(query1, keys1, values1, old_keys, old_values, fresh_open, stale_open)
    term = jnp.dot(mixed1, out_w, preferred_element_type=jnp.float32)
    summed = lax.psum_scatter(
        term.astype(jnp.bfloat16), "tp", scatter_dimension=1, tiled=True
    ).astype(jnp.float32)
    current = lax.dynamic_slice_in_dim(second, tp_index * local_width, local_width, 1)
    result = (current.astype(jnp.float32) + summed).astype(jnp.bfloat16)
    quarter = seq_len // 4

    def rows_of(block):
        return lax.dynamic_slice_in_dim(result, block * quarter, quarter, 0)

    pair = jnp.concatenate([rows_of(0), rows_of(2)], axis=0)
    pair = jnp.where(section == 1, jnp.concatenate([rows_of(1), rows_of(3)]), passed_along(pair, "section", 1))
    own_rows = lax.dynamic_slice_in_dim(pair, branch * quarter, quarter, 0)
    outbound = lax.dynamic_slice_in_dim(pair, (1 - branch) * quarter, quarter, 0)
    partner = partner_2(outbound, "cfg", 0)
    conditioned = jnp.where(branch == 0, own_rows, partner).astype(jnp.float32)
    unconditioned = jnp.where(branch == 0, partner, own_rows).astype(jnp.float32)
    guided = (unconditioned + GUIDE_SCALE * (conditioned - unconditioned)).astype(jnp.bfloat16)
    keys = jnp.where(section == 0, keys0, keys1)
    values = jnp.where(section == 0, values0, values1)
    return (guided, keys[None, None], values[None, None])


def solution(mesh):
    placed = (
        P(),
        P("cfg", None),
        P("section", None),
        P("section", None, "tp"),
        P("section", None, "tp"),
        P("section", None, "tp"),
        P("section", "tp", None),
        P("cfg", "section", None, "tp"),
        P("cfg", "section", None, "tp"),
        P(),
        P(),
    )
    return jax.shard_map(
        body,
        mesh=mesh,
        in_specs=placed,
        out_specs=(
            P(("cfg", "section"), "tp"),
            P("cfg", "section", None, "tp"),
            P("cfg", "section", None, "tp"),
        ),
        check_vma=False,
    )
```

time: 656 us -> 415 us (0.63)
  waiting for transfers between devices: 559 us -> 344 us
  other arithmetic: 30.7 us -> 15.6 us
  loops' own time: 6.95 us -> 0 us
    reduce_scatter x5 -> x1, waiting for transfers between devices: 317 us -> 116 us  [body(): lax.psum_scatter(term.astype(jnp.bfloat16), 'tp', scatter_dimension=1, ti...]
    all_gather x5 -> x2, waiting for transfers between devices: 223 us -> 182 us  [the longest x1 177 us: body(): lax.all_gather(passed_along(out_w, 'section', 1), 'tp', axis=0, tiled=True)]
    ppermute x5 -> x3, waiting for transfers between devices: 18 us -> 45.5 us  [passed_along(): return lax.ppermute(block, axis, route)]
    select_n x10 -> x1, other arithmetic: 8.64 us -> 0.09 us  [body(): jnp.where(section == 1, jnp.concatenate([rows_of(1), rows_of(3)]), passed...]
    another operation x1 -> x0, loops' own time: 6.95 us -> none  [body(): lax.fori_loop(0, ticks, advance, start)]
    dot_general x20 -> x9, matrix products: 28.7 us -> 29.4 us  [the longest x1 12.6 us: body(): summed = jnp.dot(mixed0, first_out, preferred_element_type=jnp.float32)]
  transfers between devices with their start and end apart: 16 -> 7, of which waited for: 16 -> 7; matrix products, arithmetic and copies ran while one was open for 0% -> 0% of each run, Pallas kernels for 0% -> 0%
where the time goes in v1:
time: 415 us
  waiting for transfers between devices  344 us (83%)
  matrix products  31.5 us (8%)
  other arithmetic  15.6 us (4%)
  between operations  14.1 us (3%)
  starting transfers between devices  6.76 us (2%)
    all_gather x1, waiting for transfers between devices, body(): lax.all_gather(passed_along(out_w, 'section', 1), 'tp', axis=0, tiled=True)  177 us
    reduce_scatter x1, waiting for transfers between devices, body(): lax.psum_scatter(term.astype(jnp.bfloat16), 'tp', scatter_dimension=1, ti...  116 us
    ppermute x3, waiting for transfers between devices, passed_along(): return lax.ppermute(block, axis, route)  45.5 us
    dot_general x1, matrix products, body(): summed = jnp.dot(mixed0, first_out, preferred_element_type=jnp.float32)  12.6 us
    dot_general x6, matrix products, project(): jnp.dot(normed, w, preferred_element_type=jnp.float32).astype(jnp.bfloat16)  10.8 us
  transfers between devices with their start and end apart: 7, of which 7 were waited for; matrix products, arithmetic and copies ran while one was open for 0% of the time, Pallas kernels for 0%

profile of v1, /device:TPU:0, one launch (start us, length us, event | category | flops | bytes accessed | tf_op | source)
XLA Modules:
  0.0 414.6 jit_solution(14196799117928874790)
XLA Ops:
  7.2 0.9 add.91
  8.2 5.0 %fusion.3 = f32[512]{0:T(512)S(1)} fusion(f32[6144]{0:T(1024)S(1)} %bitcast.106, bf16[512,6144]{1,0:T(8,128)(2,1)} %param.11), kind=kLoop, calls=%fused_computation.8 | loop fusion | flops 18873856 | bytes 6318080 | tf_op jit(solution)/shard_map/reduce_sum | solution.py:110
  13.3 2.6 fusion.5
  16.0 1.8 fusion.33
  17.8 1.8 fusion.39
  19.9 1.8 fusion.27
  22.0 0.4 fusion.67
  22.7 0.3 fusion.55
  23.1 0.3 fusion.46
  23.4 3.0 collective-permute-start
  26.5 3.5 collective-permute-done
  30.0 0.7 copy-done.7
  30.7 1.8 collective-permute-start.1
  32.5 34.1 %collective-permute-done.1 = bf16[128,6144]{1,0:T(8,128)(2,1)S(1)} collective-permute-done((bf16[128,6144]{1,0:T(8,128)(2,1)}, bf16[128,6144]{1,0:T(8,128)(2,1)S(1)}, u32[]{:S(2)}, u32[]{:S(2)}) %collective-permute-start.1) | collective-permute-done | bytes 1572896 | tf_op jit(solution)/shard_map/ppermute | solution.py:18
  66.6 1.2 copy-done.3
  68.0 4.3 %all-gather.3.cloned.1.call-done = bf16[512,1024]{0,1:T(8,128)(2,1)} async-done(((bf16[512,128]{0,1:T(8,128)(2,1)}), bf16[512,1024]{0,1:T(8,128)(2,1)}) %all-gather.3.cloned.1.call-update) | async-done | bytes 1048592 | tf_op jit(solution)/shard_map/all_gather | solution.py:121
  72.4 177.4 %all-gather.5.cloned.1.call-done = bf16[1024,6144]{1,0:T(8,128)(2,1)} async-done(((bf16[128,6144]{1,0:T(8,128)(2,1)}), bf16[1024,6144]{1,0:T(8,128)(2,1)}) %all-gather.5.cloned.1.call-update) | async-done | bytes 12582928 | tf_op jit(solution)/shard_map/all_gather | solution.py:105
  249.8 12.6 %fusion = (f32[512]{0:T(512)S(1)}, bf16[512,6144]{1,0:T(8,128)(2,1)S(1)}) fusion(bf16[512,1024]{0,1:T(8,128)(2,1)} %all-gather.3.cloned.1.call-done, bf16[1024,6144]{1,0:T(8,128)(2,1)} %all-gather.5.cloned.1.call-done, f32[6144]{0:T(1024)S(1)} %bitcast.108, bf16[512,6144]{1,0:T(8,128)(2,1)} %param.11), kind=kOutput, calls=%fused_computation.5 | convolution fusion | flops 6470761984 | bytes 26241024 | tf_op jit(solution)/shard_map/dot_general | solution.py:122
  262.4 2.5 fusion.2
  265.0 1.8 fusion.36
  266.9 1.8 fusion.42
  268.7 1.8 fusion.30
  270.5 0.4 fusion.69
  271.9 5.7 %convolution_convert_fusion = bf16[512,6144]{1,0:T(8,128)(2,1)} fusion(f32[128,512]{1,0:T(8,128)S(1)} %fusion.56, f32[512,512]{0,1:T(8,128)S(1)} %get-tuple-element.20, f32[512]{0:T(512)S(1)} %add.85, f32[512]{0:T(512)S(1)} %max.17, bf16[1,1,512,128]{3,2,1,0:T(8,128)(2,1)S(1)} %copy-done.4, bf16[1,128,6144]{2,1,0:T(8,128)(2,1)} %param.17), kind=kOutput, calls=%fused_computation.13 | convolution fusion | flops 876478464 | bytes 9310208 | tf_op jit(solution)/shard_map/dot_general | solution.py:134
  277.6 116.3 %reduce-scatter.2.cloned.1.call-done = bf16[512,768]{1,0:T(8,128)(2,1)} async-done(((bf16[512,6144]{1,0:T(8,128)(2,1)}), bf16[512,768]{1,0:T(8,128)(2,1)}) %reduce-scatter.2.cloned.1.call-update) | async-done | bytes 786448 | tf_op jit(solution)/shard_map/reduce_scatter | solution.py:135
  393.9 1.6 add_convert_fusion.1
  395.5 1.6 collective-permute-start.2
  397.1 0.7 select_bitcast_fusion
  397.7 7.9 %collective-permute-done.2 = bf16[256,768]{1,0:T(8,128)(2,1)S(1)} collective-permute-done((bf16[256,768]{1,0:T(8,128)(2,1)S(1)}, bf16[256,768]{1,0:T(8,128)(2,1)S(1)}, u32[]{:S(2)}, u32[]{:S(2)}) %collective-permute-start.2) | collective-permute-done | bytes 393248 | tf_op jit(solution)/shard_map/ppermute | solution.py:18
  405.9 0.7 select_bitcast_fusion.1
  406.5 0.8 collective-permute-done.3
  407.3 0.8 fusion.58
  (59 shorter events, 2.7 us)
Async XLA Ops:
  7.2 8.7 %copy-start = (bf16[1,6144,128]{2,1,0:T(8,128)(2,1)S(1)}, bf16[1,6144,128]{2,1,0:T(8,128)(2,1)}, u32[]{:S(2)}) copy-start(bf16[1,6144,128]{2,1,0:T(8,128)(2,1)} %param.14) | copy-start | bytes 4718596
  7.2 6.0 %copy-start.8 = (bf16[1,6144]{1,0:T(2,128)(2,1)S(1)}, bf16[1,6144]{1,0:T(2,128)(2,1)}, u32[]{:S(2)}) copy-start(bf16[1,6144]{1,0:T(2,128)(2,1)} %param.13) | copy-start | bytes 36868
  7.2 65.2 %all-gather.3.cloned.1.call-start = ((), (), s32[]{:S(2)}) async-start(), calls=%async_computation.1 | async-start | bytes 1179648 | tf_op jit(solution)/shard_map/all_gather | solution.py:121
  7.2 6.0 %copy-start.1 = (bf16[512,6144]{1,0:T(8,128)(2,1)S(1)}, bf16[512,6144]{1,0:T(8,128)(2,1)}, u32[]{:S(2)}) copy-start(bf16[512,6144]{1,0:T(8,128)(2,1)} %param.11) | copy-start | bytes 18874372
  15.9 1.9 copy-start.9
  15.9 3.7 copy-start.15
  15.9 3.8 copy-start.16
  16.0 3.9 copy-start.11
  19.6 2.4 copy-start.13
  21.6 1.8 copy-start.5
  21.7 1.4 copy-start.4
  23.4 6.5 %collective-permute-start = (bf16[512,128]{0,1:T(8,128)(2,1)S(1)}, bf16[512,128]{0,1:T(8,128)(2,1)S(1)}, u32[]{:S(2)}, u32[]{:S(2)}) collective-permute-start(bf16[512,128]{0,1:T(8,128)(2,1)S(1)} %fusion.46), channel_id=1, source_target_pairs={{8,0},{0,8},{9,1},{1,9},{10,2},{2,10},{11,3},{3,11},{12,4},{4,12},... | collective-permute-start | bytes 393224 | tf_op jit(solution)/shard_map/ppermute | solution.py:18
  30.0 0.7 copy-start.7
  30.7 219.1 %all-gather.5.cloned.1.call-start = ((), (), s32[]{:S(2)}) async-start(), calls=%async_computation.2 | async-start | bytes 14155776 | tf_op jit(solution)/shard_map/all_gather | solution.py:105
  30.7 35.9 %collective-permute-start.1 = (bf16[128,6144]{1,0:T(8,128)(2,1)}, bf16[128,6144]{1,0:T(8,128)(2,1)S(1)}, u32[]{:S(2)}, u32[]{:S(2)}) collective-permute-start(bf16[128,6144]{1,0:T(8,128)(2,1)} %bitcast.103), channel_id=1, source_target_pairs={{8,0},{0,8},{9,1},{1,9},{10,2},{2,10},{11,3},{3,11},{12,4},{4,12},... | collective-permute-start | bytes 4718600 | tf_op jit(solution)/shard_map/ppermute | solution.py:18
  66.6 1.2 copy-start.3
  67.8 326.1 %reduce-scatter.2.cloned.1.call-start = ((), (), s32[]{:S(2)}) async-start(), calls=%async_computation.3 | async-start | bytes 7077888 | tf_op jit(solution)/shard_map/reduce_scatter | solution.py:135
  262.4 2.6 copy-start.2
  265.0 1.8 copy-start.10
  265.0 3.6 copy-start.12
  266.9 3.6 copy-start.14
  277.6 119.5 %copy-start.6 = (bf16[512,128]{1,0:T(8,128)(2,1)S(1)}, bf16[512,128]{1,0:T(8,128)(2,1)}, u32[]{:S(2)}) copy-start(bf16[512,128]{1,0:T(8,128)(2,1)} %copy-done.5) | copy-start | bytes 393220
  395.5 10.1 %collective-permute-start.2 = (bf16[256,768]{1,0:T(8,128)(2,1)S(1)}, bf16[256,768]{1,0:T(8,128)(2,1)S(1)}, u32[]{:S(2)}, u32[]{:S(2)}) collective-permute-start(bf16[256,768]{1,0:T(8,128)(2,1)S(1)} %pad_maximum_fusion), channel_id=1, source_target_pairs={{8,0},{0,8},{9,1},{1,9},{10,2},{2,10},{11,3},{3,11},{12,4},{4,12},... | collective-permute-start | bytes 1179656 | tf_op jit(solution)/shard_map/ppermute | solution.py:18
  405.8 1.5 collective-permute-start.3
Sparse Core Ops, SparseCore 0:
  30.8 41.5 all-gather.2
  74.5 175.1 all-gather.4
  277.7 116.1 reduce-scatter.1

commit v2 on v1

--- a/solution.py
+++ b/solution.py
@@ -1,6 +1,8 @@
 import jax
 import jax.numpy as jnp
 from jax import lax
+from jax.experimental import pallas as pl
+from jax.experimental.pallas import tpu as pltpu
 from jax.sharding import PartitionSpec as P
 
 HEAD_DIM = 128
@@ -59,6 +61,294 @@
         "hrs,she->rhe", old_weight, split(old_values), preferred_element_type=jnp.float32
     )
     return mixed.reshape(row_count, head_count * HEAD_DIM).astype(jnp.bfloat16)
+
+
+GRID_X = 2
+LINE = 4
+MESH = pl.DeviceIdType.MESH
+
+
+def span(index, size):
+    return pl.ds(pl.multiple_of(index * size, size), size)
+
+
+def arrived(ref, sem):
+    pltpu.make_async_copy(ref, ref, sem).wait()
+
+
+def greet(targets):
+    barrier = pltpu.get_barrier_semaphore()
+    for target in targets:
+        pl.semaphore_signal(barrier, inc=1, device_id=target, device_id_type=MESH)
+    pl.semaphore_wait(barrier, len(targets))
+
+
+def send(src, dst, send_sem, recv_sem, target):
+    copy = pltpu.make_async_remote_copy(
+        src_ref=src,
+        dst_ref=dst,
+        send_sem=send_sem,
+        recv_sem=recv_sem,
+        device_id=target,
+        device_id_type=MESH,
+    )
+    copy.start()
+    return copy
+
+
+def share_kernel(
+    w_out,
+    w_query,
+    w_key,
+    w_value,
+    mixed,
+    wo,
+    heads,
+    proj,
+    cols,
+    wo_recv,
+    wo_send,
+    heads_recv,
+    heads_send,
+    proj_recv,
+    proj_send,
+    cols_recv,
+    cols_send,
+    edge_sem,
+    local_sem,
+):
+    c = lax.axis_index("cfg")
+    s = lax.axis_index("section")
+    t = lax.axis_index("tp")
+    tp = GRID_X * LINE
+    half = wo.shape[1]
+    part = half // 2
+    head = mixed.shape[1]
+    slim = cols.shape[1] // 2
+    across = t + 1 - 2 * lax.rem(t, 2)
+    peers = [lax.rem(t + GRID_X * k, tp) for k in range(1, LINE)]
+    sibling = {"cfg": 1 - c}
+    other = {"section": 1 - s}
+    greet([{"tp": lax.rem(t + k, tp)} for k in range(1, tp)] + [sibling, other])
+    weights = (w_query, w_key, w_value)
+
+    def wo_at(core, index):
+        return wo.at[span(index, head), span(core, part)]
+
+    def heads_at(index):
+        return heads.at[:, span(index, head)]
+
+    def cols_at(core, index):
+        return cols.at[span(index, head), span(core, slim)]
+
+    def proj_at(core, j):
+        return proj.at[span(core, part), j * head : (j + 1) * head]
+
+    def edge(j):
+        return edge_sem.at[j]
+
+    first_head = (mixed, heads_at(t))
+    first_wo = (w_out.at[:, span(c, part)], wo_at(c, t))
+
+    @pl.when(s == 0)
+    def _():
+        send(mixed, heads_at(t), edge(0), heads_recv.at[t], other)
+        send(w_out.at[:, span(c + 2, part)], wo_at(c, t), edge(1), wo_recv.at[c, t], other)
+        a = pltpu.make_async_copy(*first_head, local_sem.at[0])
+        b = pltpu.make_async_copy(*first_wo, local_sem.at[1])
+        a.start()
+        b.start()
+        a.wait()
+        b.wait()
+
+    @pl.when(s == 1)
+    def _():
+        for j, w in enumerate(weights):
+            send(w.at[span(c, part), :], proj_at(c, j), edge(j), proj_recv.at[c, j], other)
+        local = [
+            pltpu.make_async_copy(
+                w.at[half : 2 * half, :], proj.at[:, j * head : (j + 1) * head], local_sem.at[j]
+            )
+            for j, w in enumerate(weights)
+        ]
+        local += [
+            pltpu.make_async_copy(
+                w_out.at[:, pl.ds(pl.multiple_of(2 * slim * t + slim * core, slim), slim)],
+                cols_at(core, t),
+                local_sem.at[3 + core],
+            )
+            for core in range(2)
+        ]
+        for copy in local:
+            copy.start()
+        arrived(heads_at(t), heads_recv.at[t])
+        arrived(wo_at(c, t), wo_recv.at[c, t])
+        for copy in local:
+            copy.wait()
+
+    pending = []
+
+    def pass_heads(index, slot, target):
+        pending.append(
+            send(heads_at(index), heads_at(index), heads_send.at[slot], heads_recv.at[index], target)
+        )
+
+    def pass_wo(index, slot, target):
+        pending.append(
+            send(wo_at(c, index), wo_at(c, index), wo_send.at[slot], wo_recv.at[c, index], target)
+        )
+
+    for k, peer in enumerate(peers):
+        pass_heads(t, k, {"tp": peer})
+    pass_heads(t, 3, {"tp": across})
+    for k, peer in enumerate(peers):
+        pass_wo(t, k, {"tp": peer})
+    pass_wo(t, 3, {"tp": across})
+    pass_wo(t, 7, sibling)
+
+    @pl.when(s == 1)
+    def _():
+        for k in range(1, tp):
+            to = lax.rem(t + k, tp)
+            send(
+                w_out.at[:, pl.ds(pl.multiple_of(2 * slim * to + slim * c, slim), slim)],
+                cols_at(c, t),
+                cols_send.at[k],
+                cols_recv.at[c, t],
+                {"tp": to},
+            )
+
+    @pl.when(s == 0)
+    def _():
+        for j in range(3):
+            arrived(proj_at(c, j), proj_recv.at[c, j])
+            send(proj_at(c, j), proj_at(c, j), proj_send.at[j], proj_recv.at[c, j], sibling)
+
+    for k in (2, 0, 1):
+        peer = peers[k]
+        arrived(heads_at(peer), heads_recv.at[peer])
+        pass_heads(peer, 4 + k, {"tp": across})
+    for k in (2, 0, 1):
+        peer = peers[k]
+        arrived(wo_at(c, peer), wo_recv.at[c, peer])
+        pass_wo(peer, 4 + k, {"tp": across})
+        pass_wo(peer, 8 + k, sibling)
+    for k in range(LINE):
+        index = lax.rem(across + GRID_X * k, tp)
+        arrived(heads_at(index), heads_recv.at[index])
+        arrived(wo_at(c, index), wo_recv.at[c, index])
+        pass_wo(index, 11 + k, sibling)
+    for k in range(tp):
+        arrived(wo_at(1 - c, k), wo_recv.at[1 - c, k])
+
+    @pl.when(s == 0)
+    def _():
+        for j in range(3):
+            arrived(proj_at(1 - c, j), proj_recv.at[1 - c, j])
+            arrived(proj_at(c, j), proj_send.at[j])
+        arrived(mixed, edge(0))
+        arrived(w_out.at[:, span(c + 2, part)], edge(1))
+
+    @pl.when(s == 1)
+    def _():
+        for k in range(1, tp):
+            index = lax.rem(t + k, tp)
+            arrived(cols_at(c, index), cols_recv.at[c, index])
+            send(
+                cols_at(c, index),
+                cols_at(c, index),
+                cols_send.at[tp + k],
+                cols_recv.at[c, index],
+                sibling,
+            )
+        for k in range(1, tp):
+            index = lax.rem(t + k, tp)
+            arrived(cols_at(1 - c, index), cols_recv.at[1 - c, index])
+            arrived(cols_at(c, index), cols_send.at[k])
+            arrived(cols_at(c, index), cols_send.at[tp + k])
+        for j, w in enumerate(weights):
+            arrived(w.at[span(c, part), :], edge(j))
+
+    for copy in pending:
+        copy.wait_send()
+
+
+def share(w_out, w_query, w_key, w_value, mixed):
+    head, width = w_out.shape
+    tp = GRID_X * LINE
+    kind = w_out.dtype
+    DMA = pltpu.SemaphoreType.DMA
+    any_spec = pl.BlockSpec(memory_space=pl.ANY)
+    return pl.pallas_call(
+        share_kernel,
+        out_shape=(
+            jax.ShapeDtypeStruct((tp * head, width // 2), kind),
+            jax.ShapeDtypeStruct((mixed.shape[0], tp * head), kind),
+            jax.ShapeDtypeStruct((width // 2, 3 * head), kind),
+            jax.ShapeDtypeStruct((tp * head, width // tp), kind),
+        ),
+        in_specs=[any_spec] * 5,
+        out_specs=(any_spec,) * 4,
+        scratch_shapes=[
+            DMA((2, tp)),
+            DMA((16,)),
+            DMA((tp,)),
+            DMA((8,)),
+            DMA((2, 3)),
+            DMA((3,)),
+            DMA((2, tp)),
+            DMA((2 * tp,)),
+            DMA((3,)),
+            DMA((5,)),
+        ],
+        compiler_params=pltpu.CompilerParams(collective_id=0, has_side_effects=True),
+    )(w_out, w_query, w_key, w_value, mixed)
+
+
+def gather_kernel(mixed, heads, recv, sent, local_sem):
+    t = lax.axis_index("tp")
+    tp = GRID_X * LINE
+    head = mixed.shape[1]
+    across = t + 1 - 2 * lax.rem(t, 2)
+    peers = [lax.rem(t + GRID_X * k, tp) for k in range(1, LINE)]
+    greet([{"tp": p} for p in peers] + [{"tp": across}])
+
+    def heads_at(index):
+        return heads.at[:, span(index, head)]
+
+    local = pltpu.make_async_copy(mixed, heads_at(t), local_sem)
+    local.start()
+    pending = []
+    for k, peer in enumerate(peers):
+        pending.append(send(mixed, heads_at(t), sent.at[k], recv.at[t], {"tp": peer}))
+    pending.append(send(mixed, heads_at(t), sent.at[3], recv.at[t], {"tp": across}))
+    for k in (2, 0, 1):
+        peer = peers[k]
+        arrived(heads_at(peer), recv.at[peer])
+        pending.append(
+            send(heads_at(peer), heads_at(peer), sent.at[4 + k], recv.at[peer], {"tp": across})
+        )
+    for k in range(LINE):
+        index = lax.rem(across + GRID_X * k, tp)
+        arrived(heads_at(index), recv.at[index])
+    local.wait()
+    for copy in pending:
+        copy.wait_send()
+
+
+def gather_heads(mixed):
+    tp = GRID_X * LINE
+    DMA = pltpu.SemaphoreType.DMA
+    return pl.pallas_call(
+        gather_kernel,
+        out_shape=jax.ShapeDtypeStruct((mixed.shape[0], tp * mixed.shape[1]), mixed.dtype),
+        in_specs=[pl.BlockSpec(memory_space=pltpu.VMEM)],
+        out_specs=pl.BlockSpec(memory_space=pltpu.VMEM),
+        scratch_shapes=[DMA((tp,)), DMA((8,)), DMA],
+        compiler_params=pltpu.CompilerParams(
+            collective_id=1, has_side_effects=True, vmem_limit_bytes=16 * 1024 * 1024
+        ),
+    )(mixed)
 
 
 def body(
@@ -100,9 +390,7 @@
     entry = (latent.astype(jnp.float32) + condition[0].astype(jnp.float32)[None, :]).astype(
         jnp.bfloat16
     )
-    gather_weights = 2 * tp_count * out_w.shape[0] <= seq_len * 4
-    if gather_weights:
-        first_out = lax.all_gather(passed_along(out_w, "section", 1), "tp", axis=0, tiled=True)
+    planned = tp_count == GRID_X * LINE
 
     def project(rows):
         row_float = rows.astype(jnp.float32)
@@ -117,10 +405,34 @@
 
     query0, keys0, values0 = project(entry)
     mixed0 = attend_rows(query0, keys0, values0, old_keys, old_values, fresh_open, stale_open)
-    if gather_weights:
-        mixed0 = lax.all_gather(passed_along(mixed0, "section", 1), "tp", axis=1, tiled=True)
-        summed = jnp.dot(mixed0, first_out, preferred_element_type=jnp.float32)
-        second = (entry.astype(jnp.float32) + summed).astype(jnp.bfloat16)
+    if planned:
+        half = width // 2
+        later_gain = jnp.where(section == 0, passed_along(gain[0], "section", 1), gain[0])
+        half_gain = lax.dynamic_slice_in_dim(later_gain, section * half, half, 0)
+        out_half, heads0, weights_half, out_cols = share(out_w, query_w, key_w, value_w, mixed0)
+        entry_half = lax.dynamic_slice_in_dim(entry, section * half, half, 1)
+        second = (
+            entry_half.astype(jnp.float32)
+            + jnp.dot(heads0, out_half, preferred_element_type=jnp.float32)
+        ).astype(jnp.bfloat16)
+        second_float = second.astype(jnp.float32)
+        squares = jnp.sum(second_float * second_float, axis=1)
+        geared = (second_float * half_gain.astype(jnp.float32)[None, :]).astype(jnp.bfloat16)
+        partial = jnp.dot(geared, weights_half, preferred_element_type=jnp.float32)
+        far_partial = passed_along(partial.astype(jnp.bfloat16), "section", 1)
+        far_squares = passed_along(squares, "section", 1)
+        scale = lax.rsqrt((squares + far_squares) / width + NORM_EPS)
+        projected = ((partial + far_partial.astype(jnp.float32)) * scale[:, None]).astype(
+            jnp.bfloat16
+        )
+        query1, keys1, values1 = jnp.split(projected, 3, axis=1)
+        place = lax.rem(tp_index, tp_count // 2)
+        current = lax.dynamic_slice_in_dim(second, place * local_width, local_width, 1)
+        current = jnp.where(
+            tp_index < tp_count // 2, passed_along(current, "section", 1), current
+        )
+        mixed1 = attend_rows(query1, keys1, values1, old_keys, old_values, fresh_open, stale_open)
+        summed = jnp.dot(gather_heads(mixed1), out_cols, preferred_element_type=jnp.float32)
     else:
         term = jnp.dot(mixed0, out_w, preferred_element_type=jnp.float32)
         summed = lax.psum_scatter(
@@ -128,14 +440,14 @@
         ).astype(jnp.float32)
         current = lax.dynamic_slice_in_dim(entry, tp_index * local_width, local_width, 1)
         second = (current.astype(jnp.float32) + summed).astype(jnp.bfloat16)
-        second = lax.all_gather(passed_along(second, "section", 1), "tp", axis=1, tiled=True)
-    query1, keys1, values1 = project(second)
-    mixed1 = attend_rows(query1, keys1, values1, old_keys, old_values, fresh_open, stale_open)
-    term = jnp.dot(mixed1, out_w, preferred_element_type=jnp.float32)
-    summed = lax.psum_scatter(
-        term.astype(jnp.bfloat16), "tp", scatter_dimension=1, tiled=True
-    ).astype(jnp.float32)
-    current = lax.dynamic_slice_in_dim(second, tp_index * local_width, local_width, 1)
+        current = passed_along(second, "section", 1)
+        second = lax.all_gather(current, "tp", axis=1, tiled=True)
+        query1, keys1, values1 = project(second)
+        mixed1 = attend_rows(query1, keys1, values1, old_keys, old_values, fresh_open, stale_open)
+        term = jnp.dot(mixed1, out_w, preferred_element_type=jnp.float32)
+        summed = lax.psum_scatter(
+            term.astype(jnp.bfloat16), "tp", scatter_dimension=1, tiled=True
+        ).astype(jnp.float32)
     result = (current.astype(jnp.float32) + summed).astype(jnp.bfloat16)
     quarter = seq_len // 4
 

time: 415 us -> 245 us (0.59)
  waiting for transfers between devices: 344 us -> 15.5 us
  Pallas kernels: 0 us -> 111 us
  starting transfers between devices: 6.76 us -> 76 us
  between operations: 14.1 us -> 0.92 us
  matrix products: 31.5 us -> 25.3 us
    all_gather x2 -> x0, waiting for transfers between devices: 182 us -> none  [the longest x1 177 us: body(): lax.all_gather(passed_along(out_w, 'section', 1), 'tp', axis=0, tiled=True)]
    reduce_scatter x1 -> x0, waiting for transfers between devices: 116 us -> none  [body(): lax.psum_scatter(term.astype(jnp.bfloat16), 'tp', scatter_dimension=1, ti...]
    pallas_call x0 -> x2, Pallas kernels: none -> 111 us  [the longest x1 75.2 us: share(): pl.pallas_call(share_kernel, out_shape=(jax.ShapeDtypeStruct((tp * head,...]
    ppermute x3 -> x5, starting transfers between devices: 6.39 us -> 76 us  [passed_along(): return lax.ppermute(block, axis, route)]
    ppermute x3 -> x5, waiting for transfers between devices: 45.5 us -> 14.8 us  [passed_along(): return lax.ppermute(block, axis, route)]
    dot_general x6 -> x3, matrix products: 10.8 us -> 5.38 us  [project(): jnp.dot(normed, w, preferred_element_type=jnp.float32).astype(jnp.bfloat16)]
    dot_general x2 -> x3, matrix products: 18.3 us -> 15.4 us  [the longest x1 9.28 us: body(): jnp.dot(heads0, out_half, preferred_element_type=jnp.float32)]
  transfers between devices with their start and end apart: 7 -> 6, of which waited for: 7 -> 3; matrix products, arithmetic and copies ran while one was open for 0% -> 13% of each run, Pallas kernels for 0% -> 46%
where the time goes in v2:
time: 245 us; the launch traced here: 242 us
  Pallas kernels  111 us (45%)
  starting transfers between devices  76 us (31%)
  matrix products  25.3 us (10%)
  waiting for transfers between devices  15.5 us (6%)
  other arithmetic  12 us (5%)
    ppermute x5, starting transfers between devices, passed_along(): return lax.ppermute(block, axis, route)  76 us
    pallas_call x1, Pallas kernels, share(): pl.pallas_call(share_kernel, out_shape=(jax.ShapeDtypeStruct((tp * head,...  75.2 us
    pallas_call x1, Pallas kernels, gather_heads(): pl.pallas_call(gather_kernel, out_shape=jax.ShapeDtypeStruct((mixed.shape...  35.7 us
    ppermute x5, waiting for transfers between devices, passed_along(): return lax.ppermute(block, axis, route)  14.8 us
    dot_general x1, matrix products, body(): jnp.dot(heads0, out_half, preferred_element_type=jnp.float32)  9.28 us
    reduce_sum x1, other arithmetic, project(): jnp.mean(row_float * row_float, axis=1, keepdims=True) + NORM_EPS  5.44 us
    dot_general x3, matrix products, project(): jnp.dot(normed, w, preferred_element_type=jnp.float32).astype(jnp.bfloat16)  5.38 us
    dot_general x1, matrix products, body(): partial = jnp.dot(geared, weights_half, preferred_element_type=jnp.float32)  5.15 us
  transfers between devices with their start and end apart: 6, of which 3 were waited for; matrix products, arithmetic and copies ran while one was open for 13% of the time, Pallas kernels for 46%

profile of v2, /device:TPU:0, one launch (start us, length us, event | category | flops | bytes accessed | tf_op | source)
XLA Modules:
  0.0 242.3 jit_solution(11584253984726565746)
XLA Ops:
  0.6 0.8 reduce.16
  1.5 3.0 %collective-permute-start.1 = (bf16[6144]{0:T(1024)(128)(2,1)S(1)}, bf16[6144]{0:T(1024)(128)(2,1)S(1)}, u32[]{:S(2)}, u32[]{:S(2)}) collective-permute-start(bf16[6144]{0:T(1024)(128)(2,1)S(1)} %reduce.16), channel_id=1, source_target_pairs={{8,0},{0,8},{9,1},{1,9},{10,2},{2,10},{11,3},{3,11},{12,4},{4,12},... | collective-permute-start | bytes 36872 | tf_op jit(solution)/shard_map/ppermute | solution.py:20
  4.5 0.8 add.102
  5.3 5.4 %fusion = (f32[512]{0:T(512)S(1)}, bf16[512,6144]{1,0:T(8,128)(2,1)S(1)}) fusion(f32[6144]{0:T(1024)S(1)} %bitcast.77, bf16[512,6144]{1,0:T(8,128)(2,1)} %param.11), kind=kLoop, calls=%fused_computation.2 | loop fusion | flops 18873856 | bytes 12609536 | tf_op jit(solution)/shard_map/reduce_sum | solution.py:398
  10.8 2.5 %fusion.2 = bf16[512,6144]{1,0:T(8,128)(2,1)S(1)} fusion(bf16[512,6144]{1,0:T(8,128)(2,1)S(1)} %get-tuple-element.16, f32[6144]{0:T(1024)S(1)} %mul.91, f32[512]{0:T(512)S(1)} %add_rsqrt_fusion.1), kind=kLoop, calls=%fused_computation.4 | loop fusion | flops 12582912 | bytes 12609536 | tf_op jit(solution)/shard_map/convert_element_type | solution.py:400
  13.4 1.8 convolution_convert_fusion
  15.2 1.8 convolution_convert_fusion.1
  17.3 1.8 convolution_convert_fusion.2
  19.1 0.3 fusion.39
  19.4 0.4 fusion.40
  19.9 0.3 fusion.19
  20.2 0.4 fusion.22
  20.6 1.0 fusion.17.mixed
  21.6 75.2 %shard_map.130 = (bf16[1024,3072]{1,0:T(8,128)(2,1)}, bf16[512,1024]{1,0:T(8,128)(2,1)}, bf16[3072,384]{1,0:T(8,128)(2,1)}, bf16[1024,768]{1,0:T(8,128)(2,1)}) custom-call(bf16[128,6144]{1,0:T(8,128)(2,1)} %bitcast.73, bf16[6144,128]{1,0:T(8,128)(2,1)} %bitcast.74, bf16[6144,128]{1,0:T(8,128)(2,1)} %bitcast.75, bf16[6144,128]{1,0:T(8,128)(2,1)} %bitcast.76, ...), custom_call_target="tpu_custom_call" | custom-call | tf_op jit(solution)/shard_map/pallas_call | solution.py:282
  96.8 9.3 %fusion.4 = (f32[512]{0:T(512)S(1)}, bf16[512,3072]{1,0:T(8,128)(2,1)}) fusion(bf16[512,1024]{1,0:T(8,128)(2,1)} %get-tuple-element.7, bf16[1024,3072]{1,0:T(8,128)(2,1)} %get-tuple-element.8, bf16[512,6144]{1,0:T(8,128)(2,1)} %copy-done.1, s32[]{:T(128)S(6)} %select_n.81), kind=kOutput, calls=%fused_computation.9 | convolution fusion | flops 3230662144 | bytes 13633540 | tf_op jit(solution)/shard_map/dot_general | solution.py:416
  106.1 5.1 %fusion.41 = (bf16[512,384]{1,0:T(8,128)(2,1)}, f32[512,384]{1,0:T(8,128)S(1)}) fusion(bf16[3072,384]{1,0:T(8,128)(2,1)} %get-tuple-element.9, bf16[512,3072]{1,0:T(8,128)(2,1)} %get-tuple-element.30, f32[3072]{0:T(1024)S(1)} %fusion.34), kind=kOutput, calls=%fused_computation.82 | convolution fusion | flops 1212874752 | bytes 6696960 | tf_op jit(solution)/shard_map/dot_general | solution.py:421
  111.2 69.7 %collective-permute-start.2 = (bf16[512,384]{1,0:T(8,128)(2,1)}, bf16[512,384]{1,0:T(8,128)(2,1)S(1)}, u32[]{:S(2)}, u32[]{:S(2)}) collective-permute-start(bf16[512,384]{1,0:T(8,128)(2,1)} %get-tuple-element.27), channel_id=1, source_target_pairs={{8,0},{0,8},{9,1},{1,9},{10,2},{2,10},{11,3},{3,11},{12,4},{4,12},... | collective-permute-start | bytes 1179656 | tf_op jit(solution)/shard_map/ppermute | solution.py:20
  180.9 1.2 constant_dynamic-slice_fusion.1
  182.1 2.1 collective-permute-start
  184.1 6.9 %collective-permute-done.3 = f32[512]{0:T(512)S(1)} collective-permute-done((f32[512]{0:T(512)S(1)}, f32[512]{0:T(512)S(1)}, u32[]{:S(2)}, u32[]{:S(2)}) %collective-permute-start.3) | collective-permute-done | bytes 2080 | tf_op jit(solution)/shard_map/ppermute | solution.py:20
  191.2 0.4 fusion.43
  191.6 0.3 fusion.42
  192.0 0.3 fusion.21
  192.3 0.4 fusion.23
  192.7 1.3 fusion.16.mixed
  193.9 35.7 %shard_map.131 = bf16[512,1024]{1,0:T(8,128)(2,1)S(1)} custom-call(bf16[512,128]{1,0:T(8,128)(2,1)S(1)} %fusion.16.mixed), custom_call_target="tpu_custom_call" | custom-call | tf_op jit(solution)/shard_map/pallas_call | solution.py:342
  229.6 1.0 add_convert_fusion.2
  230.7 1.2 collective-permute-start.4
  231.9 7.9 %collective-permute-done.4 = bf16[256,768]{1,0:T(8,128)(2,1)S(1)} collective-permute-done((bf16[256,768]{1,0:T(8,128)(2,1)S(1)}, bf16[256,768]{1,0:T(8,128)(2,1)S(1)}, u32[]{:S(2)}, u32[]{:S(2)}) %collective-permute-start.4) | collective-permute-done | bytes 393248 | tf_op jit(solution)/shard_map/ppermute | solution.py:20
  240.1 0.7 select_bitcast_fusion
  240.8 0.7 collective-permute-done.5
  241.5 0.8 fusion.25
  (40 shorter events, 0.9 us)
Async XLA Ops:
  0.6 18.8 %copy-start = (bf16[1,1,512,128]{3,2,1,0:T(8,128)(2,1)S(1)}, bf16[1,1,512,128]{3,2,1,0:T(8,128)(2,1)}, u32[]{:S(2)}) copy-start(bf16[1,1,512,128]{3,2,1,0:T(8,128)(2,1)} %param.18) | copy-start | bytes 393220
  1.5 104.6 %collective-permute-start.1 = (bf16[6144]{0:T(1024)(128)(2,1)S(1)}, bf16[6144]{0:T(1024)(128)(2,1)S(1)}, u32[]{:S(2)}, u32[]{:S(2)}) collective-permute-start(bf16[6144]{0:T(1024)(128)(2,1)S(1)} %reduce.16), channel_id=1, source_target_pairs={{8,0},{0,8},{9,1},{1,9},{10,2},{2,10},{11,3},{3,11},{12,4},{4,12},... | collective-permute-start | bytes 36872 | tf_op jit(solution)/shard_map/ppermute | solution.py:20
  10.7 2.7 %copy-start.1 = (bf16[512,6144]{1,0:T(8,128)(2,1)}, bf16[512,6144]{1,0:T(8,128)(2,1)S(1)}, u32[]{:S(2)}) copy-start(bf16[512,6144]{1,0:T(8,128)(2,1)S(1)} %get-tuple-element.16) | copy-start | bytes 18874372
  10.8 2.7 %copy-start.3 = (bf16[1,6144,128]{2,1,0:T(8,128)(2,1)S(1)}, bf16[1,6144,128]{2,1,0:T(8,128)(2,1)}, u32[]{:S(2)}) copy-start(bf16[1,6144,128]{2,1,0:T(8,128)(2,1)} %param.15) | copy-start | bytes 4718596
  13.4 1.8 copy-start.2
  13.4 3.6 %copy-start.7 = (s32[4]{0:T(128)S(1)}, s32[4]{0:T(128)}, u32[]{:S(2)}) copy-start(s32[4]{0:T(128)} %param.20) | copy-start | bytes 52
  13.4 3.8 %copy-start.8 = (s32[4]{0:T(128)S(1)}, s32[4]{0:T(128)}, u32[]{:S(2)}) copy-start(s32[4]{0:T(128)} %param.21) | copy-start | bytes 52
  13.4 3.9 %copy-start.4 = (bf16[1,6144,128]{2,1,0:T(8,128)(2,1)S(1)}, bf16[1,6144,128]{2,1,0:T(8,128)(2,1)}, u32[]{:S(2)}) copy-start(bf16[1,6144,128]{2,1,0:T(8,128)(2,1)} %param.16) | copy-start | bytes 4718596
  19.1 1.5 copy-start.6
  111.2 79.8 %collective-permute-start.2 = (bf16[512,384]{1,0:T(8,128)(2,1)}, bf16[512,384]{1,0:T(8,128)(2,1)S(1)}, u32[]{:S(2)}, u32[]{:S(2)}) collective-permute-start(bf16[512,384]{1,0:T(8,128)(2,1)} %get-tuple-element.27), channel_id=1, source_target_pairs={{8,0},{0,8},{9,1},{1,9},{10,2},{2,10},{11,3},{3,11},{12,4},{4,12},... | collective-permute-start | bytes 1179656 | tf_op jit(solution)/shard_map/ppermute | solution.py:20
  180.9 10.2 %collective-permute-start.3 = (f32[512]{0:T(512)S(1)}, f32[512]{0:T(512)S(1)}, u32[]{:S(2)}, u32[]{:S(2)}) collective-permute-start(f32[512]{0:T(512)S(1)} %get-tuple-element.29), channel_id=1, source_target_pairs={{8,0},{0,8},{9,1},{1,9},{10,2},{2,10},{11,3},{3,11},{12,4},{4,12},... | collective-permute-start | bytes 6152 | tf_op jit(solution)/shard_map/ppermute | solution.py:20
  182.1 47.5 %collective-permute-start = (bf16[512,768]{1,0:T(8,128)(2,1)S(1)}, bf16[512,768]{1,0:T(8,128)(2,1)S(1)}, u32[]{:S(2)}, u32[]{:S(2)}) collective-permute-start(bf16[512,768]{1,0:T(8,128)(2,1)S(1)} %constant_dynamic-slice_fusion.1), channel_id=1, source_target_pairs={{8,0},{0,8},{9,1},{1,9},{10,2},{2,10},{11,3},{3,11},{12,4},{4,12},... | collective-permute-start | bytes 2359304 | tf_op jit(solution)/shard_map/ppermute | solution.py:20
  191.9 37.7 %copy-start.5 = (bf16[1024,768]{1,0:T(8,128)(2,1)S(1)}, bf16[1024,768]{1,0:T(8,128)(2,1)}, u32[]{:S(2)}) copy-start(bf16[1024,768]{1,0:T(8,128)(2,1)} %get-tuple-element.10) | copy-start | bytes 4718596
  230.7 9.1 %collective-permute-start.4 = (bf16[256,768]{1,0:T(8,128)(2,1)S(1)}, bf16[256,768]{1,0:T(8,128)(2,1)S(1)}, u32[]{:S(2)}, u32[]{:S(2)}) collective-permute-start(bf16[256,768]{1,0:T(8,128)(2,1)S(1)} %pad_maximum_fusion), channel_id=1, source_target_pairs={{8,0},{0,8},{9,1},{1,9},{10,2},{2,10},{11,3},{3,11},{12,4},{4,12},... | collective-permute-start | bytes 1179656 | tf_op jit(solution)/shard_map/ppermute | solution.py:20
  240.0 1.5 collective-permute-start.5

commit v3 on v2

--- a/solution.py
+++ b/solution.py
@@ -124,7 +124,7 @@
     half = wo.shape[1]
     part = half // 2
     head = mixed.shape[1]
-    slim = cols.shape[1] // 2
+    slim = cols.shape[2]
     across = t + 1 - 2 * lax.rem(t, 2)
     peers = [lax.rem(t + GRID_X * k, tp) for k in range(1, LINE)]
     sibling = {"cfg": 1 - c}
@@ -136,13 +136,13 @@
         return wo.at[span(index, head), span(core, part)]
 
     def heads_at(index):
-        return heads.at[:, span(index, head)]
+        return heads.at[index]
 
     def cols_at(core, index):
-        return cols.at[span(index, head), span(core, slim)]
+        return cols.at[core, span(index, head), :]
 
     def proj_at(core, j):
-        return proj.at[span(core, part), j * head : (j + 1) * head]
+        return proj.at[j, span(core, part), :]
 
     def edge(j):
         return edge_sem.at[j]
@@ -161,17 +161,14 @@
         a.wait()
         b.wait()
 
-    @pl.when(s == 1)
-    def _():
-        for j, w in enumerate(weights):
-            send(w.at[span(c, part), :], proj_at(c, j), edge(j), proj_recv.at[c, j], other)
-        local = [
+    def own_copies():
+        copies = [
             pltpu.make_async_copy(
-                w.at[half : 2 * half, :], proj.at[:, j * head : (j + 1) * head], local_sem.at[j]
+                w.at[half : 2 * half, :], proj.at[j], local_sem.at[j]
             )
             for j, w in enumerate(weights)
         ]
-        local += [
+        copies += [
             pltpu.make_async_copy(
                 w_out.at[:, pl.ds(pl.multiple_of(2 * slim * t + slim * core, slim), slim)],
                 cols_at(core, t),
@@ -179,35 +176,12 @@
             )
             for core in range(2)
         ]
-        for copy in local:
-            copy.start()
-        arrived(heads_at(t), heads_recv.at[t])
-        arrived(wo_at(c, t), wo_recv.at[c, t])
-        for copy in local:
-            copy.wait()
-
-    pending = []
-
-    def pass_heads(index, slot, target):
-        pending.append(
-            send(heads_at(index), heads_at(index), heads_send.at[slot], heads_recv.at[index], target)
-        )
-
-    def pass_wo(index, slot, target):
-        pending.append(
-            send(wo_at(c, index), wo_at(c, index), wo_send.at[slot], wo_recv.at[c, index], target)
-        )
-
-    for k, peer in enumerate(peers):
-        pass_heads(t, k, {"tp": peer})
-    pass_heads(t, 3, {"tp": across})
-    for k, peer in enumerate(peers):
-        pass_wo(t, k, {"tp": peer})
-    pass_wo(t, 3, {"tp": across})
-    pass_wo(t, 7, sibling)
+        return copies
 
     @pl.when(s == 1)
     def _():
+        for j, w in enumerate(weights):
+            send(w.at[span(c, part), :], proj_at(c, j), edge(j), proj_recv.at[c, j], other)
         for k in range(1, tp):
             to = lax.rem(t + k, tp)
             send(
@@ -217,12 +191,30 @@
                 cols_recv.at[c, t],
                 {"tp": to},
             )
-
-    @pl.when(s == 0)
-    def _():
-        for j in range(3):
-            arrived(proj_at(c, j), proj_recv.at[c, j])
-            send(proj_at(c, j), proj_at(c, j), proj_send.at[j], proj_recv.at[c, j], sibling)
+        for copy in own_copies():
+            copy.start()
+        arrived(heads_at(t), heads_recv.at[t])
+        arrived(wo_at(c, t), wo_recv.at[c, t])
+
+    pending = []
+
+    def pass_heads(index, slot, target):
+        pending.append(
+            send(heads_at(index), heads_at(index), heads_send.at[slot], heads_recv.at[index], target)
+        )
+
+    def pass_wo(index, slot, target):
+        pending.append(
+            send(wo_at(c, index), wo_at(c, index), wo_send.at[slot], wo_recv.at[c, index], target)
+        )
+
+    for k, peer in enumerate(peers):
+        pass_heads(t, k, {"tp": peer})
+    pass_heads(t, 3, {"tp": across})
+    for k, peer in enumerate(peers):
+        pass_wo(t, k, {"tp": peer})
+    pass_wo(t, 3, {"tp": across})
+    pass_wo(t, 7, sibling)
 
     for k in (2, 0, 1):
         peer = peers[k]
@@ -238,11 +230,12 @@
         arrived(heads_at(index), heads_recv.at[index])
         arrived(wo_at(c, index), wo_recv.at[c, index])
         pass_wo(index, 11 + k, sibling)
-    for k in range(tp):
-        arrived(wo_at(1 - c, k), wo_recv.at[1 - c, k])
 
     @pl.when(s == 0)
     def _():
+        for j in range(3):
+            arrived(proj_at(c, j), proj_recv.at[c, j])
+            send(proj_at(c, j), proj_at(c, j), proj_send.at[j], proj_recv.at[c, j], sibling)
         for j in range(3):
             arrived(proj_at(1 - c, j), proj_recv.at[1 - c, j])
             arrived(proj_at(c, j), proj_send.at[j])
@@ -268,7 +261,11 @@
             arrived(cols_at(c, index), cols_send.at[tp + k])
         for j, w in enumerate(weights):
             arrived(w.at[span(c, part), :], edge(j))
-
+        for copy in own_copies():
+            copy.wait()
+
+    for k in range(tp):
+        arrived(wo_at(1 - c, k), wo_recv.at[1 - c, k])
     for copy in pending:
         copy.wait_send()
 
@@ -283,9 +280,9 @@
         share_kernel,
         out_shape=(
             jax.ShapeDtypeStruct((tp * head, width // 2), kind),
-            jax.ShapeDtypeStruct((mixed.shape[0], tp * head), kind),
-            jax.ShapeDtypeStruct((width // 2, 3 * head), kind),
-            jax.ShapeDtypeStruct((tp * head, width // tp), kind),
+            jax.ShapeDtypeStruct((tp,) + mixed.shape, kind),
+            jax.ShapeDtypeStruct((3, width // 2, head), kind),
+            jax.ShapeDtypeStruct((2, tp * head, width // tp // 2), kind),
         ),
         in_specs=[any_spec] * 5,
         out_specs=(any_spec,) * 4,
@@ -413,12 +410,19 @@
         entry_half = lax.dynamic_slice_in_dim(entry, section * half, half, 1)
         second = (
             entry_half.astype(jnp.float32)
-            + jnp.dot(heads0, out_half, preferred_element_type=jnp.float32)
+            + jnp.dot(
+                heads0.transpose(1, 0, 2).reshape(seq_len, tp_count * HEAD_DIM),
+                out_half,
+                preferred_element_type=jnp.float32,
+            )
         ).astype(jnp.bfloat16)
         second_float = second.astype(jnp.float32)
         squares = jnp.sum(second_float * second_float, axis=1)
         geared = (second_float * half_gain.astype(jnp.float32)[None, :]).astype(jnp.bfloat16)
-        partial = jnp.dot(geared, weights_half, preferred_element_type=jnp.float32)
+        partial = jnp.concatenate(
+            [jnp.dot(geared, weights_half[j], preferred_element_type=jnp.float32) for j in range(3)],
+            axis=1,
+        )
         far_partial = passed_along(partial.astype(jnp.bfloat16), "section", 1)
         far_squares = passed_along(squares, "section", 1)
         scale = lax.rsqrt((squares + far_squares) / width + NORM_EPS)
@@ -432,7 +436,30 @@
             tp_index < tp_count // 2, passed_along(current, "section", 1), current
         )
         mixed1 = attend_rows(query1, keys1, values1, old_keys, old_values, fresh_open, stale_open)
-        summed = jnp.dot(gather_heads(mixed1), out_cols, preferred_element_type=jnp.float32)
+        rows = seq_len // 2
+
+        def both(array):
+            mine = lax.dynamic_slice_in_dim(array, branch * rows, rows, 0)
+            away = lax.dynamic_slice_in_dim(array, (1 - branch) * rows, rows, 0)
+            away = partner_2(away, "cfg", 0).astype(jnp.float32)
+            mine = mine.astype(jnp.float32)
+            cond = jnp.where(branch == 0, mine, away)
+            uncond = jnp.where(branch == 0, away, mine)
+            return uncond + GUIDE_SCALE * (cond - uncond)
+
+        base = both(current)
+        heads1 = gather_heads(both(mixed1).astype(jnp.bfloat16))
+        summed = jnp.concatenate(
+            [jnp.dot(heads1, out_cols[k], preferred_element_type=jnp.float32) for k in range(2)],
+            axis=1,
+        )
+        result = (base + summed).astype(jnp.bfloat16)
+        guided = jnp.where(
+            section == 0, passed_along(result[: rows // 2], "section", 1), result[rows // 2 :]
+        )
+        keys = jnp.where(section == 0, keys0, keys1)
+        values = jnp.where(section == 0, values0, values1)
+        return (guided, keys[None, None], values[None, None])
     else:
         term = jnp.dot(mixed0, out_w, preferred_element_type=jnp.float32)
         summed = lax.psum_scatter(

time: 245 us -> 169 us (0.69)
  starting transfers between devices: 76 us -> 13 us
  Pallas kernels: 111 us -> 96.9 us
    ppermute x5, starting transfers between devices: 76 us -> 12.9 us  [passed_along(): return lax.ppermute(block, axis, route)]
    pallas_call x1, Pallas kernels: 35.7 us -> 20 us  [gather_heads(): pl.pallas_call(gather_kernel, out_shape=jax.ShapeDtypeStruct((mixed.shape...]
    dot_general x3 -> x6, matrix products: 15.4 us -> 17.1 us  [the longest x1 8.75 us: body(): jnp.dot(heads0.transpose(1, 0, 2).reshape(seq_len, tp_count * HEAD_DIM),...]
  transfers between devices with their start and end apart: 6 -> 7, of which waited for: 3 -> 3; matrix products, arithmetic and copies ran while one was open for 13% -> 20% of each run, Pallas kernels for 46% -> 57%
where the time goes in v3:
time: 169 us
  Pallas kernels  96.9 us (57%)
  matrix products  26.1 us (15%)
  waiting for transfers between devices  14.5 us (9%)
  other arithmetic  13.5 us (8%)
  starting transfers between devices  13 us (8%)
  local copies, waits for them, and re-layouts  3.63 us (2%)
    pallas_call x1, Pallas kernels, share(): pl.pallas_call(share_kernel, out_shape=(jax.ShapeDtypeStruct((tp * head,...  76.9 us
    pallas_call x1, Pallas kernels, gather_heads(): pl.pallas_call(gather_kernel, out_shape=jax.ShapeDtypeStruct((mixed.shape...  20 us
    ppermute x5, waiting for transfers between devices, passed_along(): return lax.ppermute(block, axis, route)  13.3 us
    ppermute x5, starting transfers between devices, passed_along(): return lax.ppermute(block, axis, route)  12.9 us
    dot_general x1, matrix products, body(): jnp.dot(heads0.transpose(1, 0, 2).reshape(seq_len, tp_count * HEAD_DIM),...  8.75 us
    reduce_sum x1, other arithmetic, project(): jnp.mean(row_float * row_float, axis=1, keepdims=True) + NORM_EPS  5.47 us
    dot_general x3, matrix products, project(): jnp.dot(normed, w, preferred_element_type=jnp.float32).astype(jnp.bfloat16)  5.39 us
    dot_general x3, matrix products, body(): jnp.dot(geared, weights_half[j], preferred_element_type=jnp.float32)  5.18 us
  transfers between devices with their start and end apart: 7, of which 3 were waited for; matrix products, arithmetic and copies ran while one was open for 20% of the time, Pallas kernels for 57%

profile of v3, /device:TPU:0, one launch (start us, length us, event | category | flops | bytes accessed | tf_op | source)
XLA Modules:
  0.0 168.6 jit_solution(4571308136720563926)
XLA Ops:
  0.6 0.8 reduce.16
  1.5 3.0 %collective-permute-start.2 = (bf16[6144]{0:T(1024)(128)(2,1)S(1)}, bf16[6144]{0:T(1024)(128)(2,1)S(1)}, u32[]{:S(2)}, u32[]{:S(2)}) collective-permute-start(bf16[6144]{0:T(1024)(128)(2,1)S(1)} %reduce.16), channel_id=1, source_target_pairs={{8,0},{0,8},{9,1},{1,9},{10,2},{2,10},{11,3},{3,11},{12,4},{4,12},... | collective-permute-start | bytes 36872 | tf_op jit(solution)/shard_map/ppermute | solution.py:20
  4.5 0.8 add.108
  5.3 5.5 %fusion = (f32[512]{0:T(512)S(1)}, bf16[512,6144]{1,0:T(8,128)(2,1)S(1)}) fusion(f32[6144]{0:T(1024)S(1)} %bitcast.100, bf16[512,6144]{1,0:T(8,128)(2,1)} %param.11), kind=kLoop, calls=%fused_computation.2 | loop fusion | flops 18873856 | bytes 12609536 | tf_op jit(solution)/shard_map/reduce_sum | solution.py:395
  10.8 2.5 %fusion.2 = bf16[512,6144]{1,0:T(8,128)(2,1)S(1)} fusion(bf16[512,6144]{1,0:T(8,128)(2,1)S(1)} %get-tuple-element.16, f32[6144]{0:T(1024)S(1)} %mul.99, f32[512]{0:T(512)S(1)} %add_rsqrt_fusion.1), kind=kLoop, calls=%fused_computation.4 | loop fusion | flops 12582912 | bytes 12609536 | tf_op jit(solution)/shard_map/convert_element_type | solution.py:397
  13.5 1.8 %convolution_convert_fusion = bf16[512,128]{1,0:T(8,128)(2,1)S(1)} fusion(bf16[512,6144]{1,0:T(8,128)(2,1)S(1)} %fusion.2, bf16[1,6144,128]{2,1,0:T(8,128)(2,1)S(1)} %copy-done.3), kind=kOutput, calls=%fused_computation.28 | convolution fusion | flops 805371904 | bytes 7995392 | tf_op jit(solution)/shard_map/dot_general | solution.py:399
  15.3 1.8 %convolution_convert_fusion.1 = bf16[512,128]{1,0:T(8,128)(2,1)S(1)} fusion(bf16[512,6144]{1,0:T(8,128)(2,1)S(1)} %fusion.2, bf16[1,6144,128]{2,1,0:T(8,128)(2,1)S(1)} %copy-done.2), kind=kOutput, calls=%fused_computation.29 | convolution fusion | flops 805371904 | bytes 7995392 | tf_op jit(solution)/shard_map/dot_general | solution.py:399
  17.3 1.8 %convolution_convert_fusion.2 = bf16[512,128]{1,0:T(8,128)(2,1)S(1)} fusion(bf16[512,6144]{1,0:T(8,128)(2,1)S(1)} %fusion.2, bf16[1,6144,128]{2,1,0:T(8,128)(2,1)S(1)} %copy-done.4), kind=kOutput, calls=%fused_computation.30 | convolution fusion | flops 805371904 | bytes 7995392 | tf_op jit(solution)/shard_map/dot_general | solution.py:399
  19.5 0.4 fusion.61
  20.2 0.4 fusion.42
  20.6 1.0 fusion.19.mixed
  21.6 76.9 %shard_map.130 = (bf16[1024,3072]{1,0:T(8,128)(2,1)}, bf16[8,512,128]{2,1,0:T(8,128)(2,1)}, bf16[3,3072,128]{2,1,0:T(8,128)(2,1)}, bf16[2,1024,384]{2,1,0:T(8,128)(2,1)}) custom-call(bf16[128,6144]{1,0:T(8,128)(2,1)} %bitcast.94, bf16[6144,128]{1,0:T(8,128)(2,1)} %bitcast.95, bf16[6144,128]{1,0:T(8,128)(2,1)} %bitcast.96, bf16[6144,128]{1,0:T(8,128)(2,1)} %bitcast.97, ...), custom_call_target="tpu_custom_call" | custom-call | tf_op jit(solution)/shard_map/pallas_call | solution.py:279
  98.6 1.5 copy.26
  100.1 8.8 %fusion.4 = (f32[512]{0:T(512)S(1)}, bf16[512,3072]{1,0:T(8,128)(2,1)}) fusion(bf16[512,1024]{0,1:T(8,128)(2,1)S(1)} %bitcast.98, bf16[1024,3072]{1,0:T(8,128)(2,1)} %get-tuple-element.8, bf16[512,6144]{1,0:T(8,128)(2,1)} %copy-done.1, s32[]{:T(128)S(6)} %select_n.95), kind=kOutput, calls=%fused_computation.9 | convolution fusion | flops 3230662144 | bytes 13633540 | tf_op jit(solution)/shard_map/dot_general | solution.py:413
  108.8 3.2 %fusion.9 = f32[512,128]{1,0:T(8,128)S(1)} fusion(bf16[512,3072]{1,0:T(8,128)(2,1)} %get-tuple-element.24, f32[3072]{0:T(1024)S(1)} %fusion.56, bf16[3,3072,128]{2,1,0:T(8,128)(2,1)} %get-tuple-element.9), kind=kOutput, calls=%fused_computation.13 | convolution fusion | flops 407371776 | bytes 4206592 | tf_op jit(solution)/shard_map/dot_general | solution.py:423
  112.1 0.5 copy-done.6
  112.6 1.0 fusion.7
  113.6 1.0 fusion.5
  114.6 7.6 %collective-permute-start.3 = (bf16[512,384]{1,0:T(8,128)(2,1)S(1)}, bf16[512,384]{1,0:T(8,128)(2,1)S(1)}, u32[]{:S(2)}, u32[]{:S(2)}) collective-permute-start(bf16[512,384]{1,0:T(8,128)(2,1)S(1)} %fusion.41), channel_id=1, source_target_pairs={{8,0},{0,8},{9,1},{1,9},{10,2},{2,10},{11,3},{3,11},{12,4},{4,12},... | collective-permute-start | bytes 1179656 | tf_op jit(solution)/shard_map/ppermute | solution.py:20
  122.4 1.2 constant_dynamic-slice_fusion.1
  123.5 2.0 %collective-permute-start = (bf16[512,768]{1,0:T(8,128)(2,1)S(1)}, bf16[512,768]{1,0:T(8,128)(2,1)S(1)}, u32[]{:S(2)}, u32[]{:S(2)}) collective-permute-start(bf16[512,768]{1,0:T(8,128)(2,1)S(1)} %constant_dynamic-slice_fusion.1), channel_id=1, source_target_pairs={{8,0},{0,8},{9,1},{1,9},{10,2},{2,10},{11,3},{3,11},{12,4},{4,12},... | collective-permute-start | bytes 2359304 | tf_op jit(solution)/shard_map/ppermute | solution.py:20
  125.6 6.8 %collective-permute-done.4 = f32[512]{0:T(512)S(1)} collective-permute-done((f32[512]{0:T(512)S(1)}, f32[512]{0:T(512)S(1)}, u32[]{:S(2)}, u32[]{:S(2)}) %collective-permute-start.4) | collective-permute-done | bytes 2080 | tf_op jit(solution)/shard_map/ppermute | solution.py:20
  132.5 0.4 fusion.63
  133.6 0.4 fusion.43
  134.5 1.2 collective-permute-done.5
  135.7 20.0 %shard_map.131 = bf16[256,1024]{1,0:T(8,128)(2,1)S(1)} custom-call(bf16[256,128]{1,0:T(8,128)(2,1)S(1)} %fusion.47.mixed), custom_call_target="tpu_custom_call" | custom-call | tf_op jit(solution)/shard_map/pallas_call | solution.py:339
  155.7 1.3 broadcast_select_fusion
  157.2 1.6 fusion.31
  158.7 1.6 fusion.29
  160.7 0.7 select_bitcast_fusion
  161.4 6.5 %collective-permute-done.6 = bf16[128,768]{1,0:T(8,128)(2,1)S(1)} collective-permute-done((bf16[128,768]{1,0:T(8,128)(2,1)S(1)}, bf16[128,768]{1,0:T(8,128)(2,1)S(1)}, u32[]{:S(2)}, u32[]{:S(2)}) %collective-permute-start.6) | collective-permute-done | bytes 196640 | tf_op jit(solution)/shard_map/ppermute | solution.py:20
  167.9 0.7 slice_select_fusion
  (53 shorter events, 3.0 us)
Async XLA Ops:
  0.6 18.8 %copy-start = (bf16[1,1,512,128]{3,2,1,0:T(8,128)(2,1)S(1)}, bf16[1,1,512,128]{3,2,1,0:T(8,128)(2,1)}, u32[]{:S(2)}) copy-start(bf16[1,1,512,128]{3,2,1,0:T(8,128)(2,1)} %param.18) | copy-start | bytes 393220
  1.5 107.3 %collective-permute-start.2 = (bf16[6144]{0:T(1024)(128)(2,1)S(1)}, bf16[6144]{0:T(1024)(128)(2,1)S(1)}, u32[]{:S(2)}, u32[]{:S(2)}) collective-permute-start(bf16[6144]{0:T(1024)(128)(2,1)S(1)} %reduce.16), channel_id=1, source_target_pairs={{8,0},{0,8},{9,1},{1,9},{10,2},{2,10},{11,3},{3,11},{12,4},{4,12},... | collective-permute-start | bytes 36872 | tf_op jit(solution)/shard_map/ppermute | solution.py:20
  10.8 2.7 %copy-start.1 = (bf16[512,6144]{1,0:T(8,128)(2,1)}, bf16[512,6144]{1,0:T(8,128)(2,1)S(1)}, u32[]{:S(2)}) copy-start(bf16[512,6144]{1,0:T(8,128)(2,1)S(1)} %get-tuple-element.16) | copy-start | bytes 18874372
  10.8 2.7 %copy-start.3 = (bf16[1,6144,128]{2,1,0:T(8,128)(2,1)S(1)}, bf16[1,6144,128]{2,1,0:T(8,128)(2,1)}, u32[]{:S(2)}) copy-start(bf16[1,6144,128]{2,1,0:T(8,128)(2,1)} %param.15) | copy-start | bytes 4718596
  13.4 1.8 %copy-start.2 = (bf16[1,6144,128]{2,1,0:T(8,128)(2,1)S(1)}, bf16[1,6144,128]{2,1,0:T(8,128)(2,1)}, u32[]{:S(2)}) copy-start(bf16[1,6144,128]{2,1,0:T(8,128)(2,1)} %param.14) | copy-start | bytes 4718596
  13.4 3.6 %copy-start.9 = (s32[4]{0:T(128)S(1)}, s32[4]{0:T(128)}, u32[]{:S(2)}) copy-start(s32[4]{0:T(128)} %param.20) | copy-start | bytes 52
  13.4 3.8 %copy-start.10 = (s32[4]{0:T(128)S(1)}, s32[4]{0:T(128)}, u32[]{:S(2)}) copy-start(s32[4]{0:T(128)} %param.21) | copy-start | bytes 52
  13.5 3.9 %copy-start.4 = (bf16[1,6144,128]{2,1,0:T(8,128)(2,1)S(1)}, bf16[1,6144,128]{2,1,0:T(8,128)(2,1)}, u32[]{:S(2)}) copy-start(bf16[1,6144,128]{2,1,0:T(8,128)(2,1)} %param.16) | copy-start | bytes 4718596
  19.1 1.5 copy-start.7
  108.8 3.3 %copy-start.5 = (bf16[512,3072]{1,0:T(8,128)(2,1)S(1)}, bf16[512,3072]{1,0:T(8,128)(2,1)}, u32[]{:S(2)}) copy-start(bf16[512,3072]{1,0:T(8,128)(2,1)} %get-tuple-element.24) | copy-start | bytes 9437188
  108.8 3.8 %copy-start.6 = (bf16[3,3072,128]{2,1,0:T(8,128)(2,1)S(1)}, bf16[3,3072,128]{2,1,0:T(8,128)(2,1)}, u32[]{:S(2)}) copy-start(bf16[3,3072,128]{2,1,0:T(8,128)(2,1)} %get-tuple-element.9) | copy-start | bytes 7077892
  114.6 17.7 %collective-permute-start.3 = (bf16[512,384]{1,0:T(8,128)(2,1)S(1)}, bf16[512,384]{1,0:T(8,128)(2,1)S(1)}, u32[]{:S(2)}, u32[]{:S(2)}) collective-permute-start(bf16[512,384]{1,0:T(8,128)(2,1)S(1)} %fusion.41), channel_id=1, source_target_pairs={{8,0},{0,8},{9,1},{1,9},{10,2},{2,10},{11,3},{3,11},{12,4},{4,12},... | collective-permute-start | bytes 1179656 | tf_op jit(solution)/shard_map/ppermute | solution.py:20
  122.3 10.1 %collective-permute-start.4 = (f32[512]{0:T(512)S(1)}, f32[512]{0:T(512)S(1)}, u32[]{:S(2)}, u32[]{:S(2)}) collective-permute-start(f32[512]{0:T(512)S(1)} %get-tuple-element.23), channel_id=1, source_target_pairs={{8,0},{0,8},{9,1},{1,9},{10,2},{2,10},{11,3},{3,11},{12,4},{4,12},... | collective-permute-start | bytes 6152 | tf_op jit(solution)/shard_map/ppermute | solution.py:20
  123.5 32.2 %collective-permute-start = (bf16[512,768]{1,0:T(8,128)(2,1)S(1)}, bf16[512,768]{1,0:T(8,128)(2,1)S(1)}, u32[]{:S(2)}, u32[]{:S(2)}) collective-permute-start(bf16[512,768]{1,0:T(8,128)(2,1)S(1)} %constant_dynamic-slice_fusion.1), channel_id=1, source_target_pairs={{8,0},{0,8},{9,1},{1,9},{10,2},{2,10},{11,3},{3,11},{12,4},{4,12},... | collective-permute-start | bytes 2359304 | tf_op jit(solution)/shard_map/ppermute | solution.py:20
  125.6 8.4 %copy-start.8 = (bf16[1,1,512,128]{3,2,1,0:T(8,128)(2,1)S(1)}, bf16[1,1,512,128]{3,2,1,0:T(8,128)(2,1)}, u32[]{:S(2)}) copy-start(bf16[1,1,512,128]{3,2,1,0:T(8,128)(2,1)} %param.19) | copy-start | bytes 393220
  134.4 1.3 collective-permute-start.5
  157.1 3.2 %collective-permute-start.1 = (bf16[256,768]{1,0:T(8,128)(2,1)S(1)}, bf16[256,768]{1,0:T(8,128)(2,1)S(1)}, u32[]{:S(2)}, u32[]{:S(2)}) collective-permute-start(bf16[256,768]{1,0:T(8,128)(2,1)S(1)} %constant_dynamic-slice_fusion), channel_id=1, source_target_pairs={{0,16},{16,0},{1,17},{17,1},{2,18},{18,2},{3,19},{19,3},{4,20},{20... | collective-permute-start | bytes 1179656 | tf_op jit(solution)/shard_map/ppermute | solution.py:24
  160.6 7.4 %collective-permute-start.6 = (bf16[128,768]{1,0:T(8,128)(2,1)S(1)}, bf16[128,768]{1,0:T(8,128)(2,1)S(1)}, u32[]{:S(2)}, u32[]{:S(2)}) collective-permute-start(bf16[128,768]{1,0:T(8,128)(2,1)S(1)} %slice.28), channel_id=1, source_target_pairs={{8,0},{0,8},{9,1},{1,9},{10,2},{2,10},{11,3},{3,11},{12,4},{4,12},... | collective-permute-start | bytes 589832 | tf_op jit(solution)/shard_map/ppermute | solution.py:20

commit v4 on v3

--- a/solution.py
+++ b/solution.py
@@ -65,6 +65,7 @@
 
 GRID_X = 2
 LINE = 4
+CUTS = 4
 MESH = pl.DeviceIdType.MESH
 
 
@@ -135,6 +136,11 @@
     def wo_at(core, index):
         return wo.at[span(index, head), span(core, part)]
 
+    piece = part // CUTS
+
+    def wo_cut(core, index, cut):
+        return wo.at[span(index, head), span(core * CUTS + cut, piece)]
+
     def heads_at(index):
         return heads.at[index]
 
@@ -153,7 +159,14 @@
     @pl.when(s == 0)
     def _():
         send(mixed, heads_at(t), edge(0), heads_recv.at[t], other)
-        send(w_out.at[:, span(c + 2, part)], wo_at(c, t), edge(1), wo_recv.at[c, t], other)
+        for cut in range(CUTS):
+            send(
+                w_out.at[:, span((c + 2) * CUTS + cut, piece)],
+                wo_cut(c, t, cut),
+                edge(1 + cut),
+                wo_recv.at[c, t, cut],
+                other,
+            )
         a = pltpu.make_async_copy(*first_head, local_sem.at[0])
         b = pltpu.make_async_copy(*first_wo, local_sem.at[1])
         a.start()
@@ -194,7 +207,6 @@
         for copy in own_copies():
             copy.start()
         arrived(heads_at(t), heads_recv.at[t])
-        arrived(wo_at(c, t), wo_recv.at[c, t])
 
     pending = []
 
@@ -203,33 +215,56 @@
             send(heads_at(index), heads_at(index), heads_send.at[slot], heads_recv.at[index], target)
         )
 
-    def pass_wo(index, slot, target):
+    def pass_wo(index, slot, cut, target):
         pending.append(
-            send(wo_at(c, index), wo_at(c, index), wo_send.at[slot], wo_recv.at[c, index], target)
-        )
+            send(
+                wo_cut(c, index, cut),
+                wo_cut(c, index, cut),
+                wo_send.at[slot, cut],
+                wo_recv.at[c, index, cut],
+                target,
+            )
+        )
+
+    def take_wo(index, cut):
+        arrived(wo_cut(c, index, cut), wo_recv.at[c, index, cut])
 
     for k, peer in enumerate(peers):
         pass_heads(t, k, {"tp": peer})
     pass_heads(t, 3, {"tp": across})
-    for k, peer in enumerate(peers):
-        pass_wo(t, k, {"tp": peer})
-    pass_wo(t, 3, {"tp": across})
-    pass_wo(t, 7, sibling)
-
+    for cut in range(CUTS):
+
+        @pl.when(s == 1)
+        def _():
+            take_wo(t, cut)
+
+        pass_wo(t, 3, cut, {"tp": across})
+        for k, peer in enumerate(peers):
+            pass_wo(t, k, cut, {"tp": peer})
     for k in (2, 0, 1):
         peer = peers[k]
         arrived(heads_at(peer), heads_recv.at[peer])
         pass_heads(peer, 4 + k, {"tp": across})
-    for k in (2, 0, 1):
-        peer = peers[k]
-        arrived(wo_at(c, peer), wo_recv.at[c, peer])
-        pass_wo(peer, 4 + k, {"tp": across})
-        pass_wo(peer, 8 + k, sibling)
+
+    def finish(cut):
+        for k in range(LINE):
+            index = lax.rem(across + GRID_X * k, tp)
+            take_wo(index, cut)
+            pass_wo(index, 11 + k, cut, sibling)
+
+    for cut in range(CUTS):
+        for k in (2, 0, 1):
+            take_wo(peers[k], cut)
+            pass_wo(peers[k], 4 + k, cut, {"tp": across})
+        pass_wo(t, 7, cut, sibling)
+        for k in range(LINE - 1):
+            pass_wo(peers[k], 8 + k, cut, sibling)
+        if cut > 0:
+            finish(cut - 1)
+    finish(CUTS - 1)
     for k in range(LINE):
         index = lax.rem(across + GRID_X * k, tp)
         arrived(heads_at(index), heads_recv.at[index])
-        arrived(wo_at(c, index), wo_recv.at[c, index])
-        pass_wo(index, 11 + k, sibling)
 
     @pl.when(s == 0)
     def _():
@@ -240,7 +275,8 @@
             arrived(proj_at(1 - c, j), proj_recv.at[1 - c, j])
             arrived(proj_at(c, j), proj_send.at[j])
         arrived(mixed, edge(0))
-        arrived(w_out.at[:, span(c + 2, part)], edge(1))
+        for cut in range(CUTS):
+            arrived(wo_cut(c, t, cut), edge(1 + cut))
 
     @pl.when(s == 1)
     def _():
@@ -265,7 +301,8 @@
             copy.wait()
 
     for k in range(tp):
-        arrived(wo_at(1 - c, k), wo_recv.at[1 - c, k])
+        for cut in range(CUTS):
+            arrived(wo_cut(1 - c, k, cut), wo_recv.at[1 - c, k, cut])
     for copy in pending:
         copy.wait_send()
 
@@ -287,15 +324,15 @@
         in_specs=[any_spec] * 5,
         out_specs=(any_spec,) * 4,
         scratch_shapes=[
-            DMA((2, tp)),
-            DMA((16,)),
+            DMA((2, tp, CUTS)),
+            DMA((16, CUTS)),
             DMA((tp,)),
             DMA((8,)),
             DMA((2, 3)),
             DMA((3,)),
             DMA((2, tp)),
             DMA((2 * tp,)),
-            DMA((3,)),
+            DMA((max(3, 1 + CUTS),)),
             DMA((5,)),
         ],
         compiler_params=pltpu.CompilerParams(collective_id=0, has_side_effects=True),

time: 169 us -> 163 us (0.964)
  Pallas kernels: 96.9 us -> 90.9 us
  starting transfers between devices: 13 us -> 15 us
    pallas_call x1, Pallas kernels: 20 us -> 13.1 us  [gather_heads(): pl.pallas_call(gather_kernel, out_shape=jax.ShapeDtypeStruct((mixed.shape...]
    ppermute x5, starting transfers between devices: 12.9 us -> 14.9 us  [passed_along(): return lax.ppermute(block, axis, route)]
  transfers between devices with their start and end apart: 7 -> 7, of which waited for: 3 -> 3; matrix products, arithmetic and copies ran while one was open for 20% -> 21% of each run, Pallas kernels for 57% -> 56%
where the time goes in v4:
time: 163 us
  Pallas kernels  90.9 us (56%)
  matrix products  26 us (16%)
  starting transfers between devices  15 us (9%)
  other arithmetic  13.5 us (8%)
  waiting for transfers between devices  12.9 us (8%)
  local copies, waits for them, and re-layouts  3.63 us (2%)
    pallas_call x1, Pallas kernels, share(): pl.pallas_call(share_kernel, out_shape=(jax.ShapeDtypeStruct((tp * head,...  77.8 us
    ppermute x5, starting transfers between devices, passed_along(): return lax.ppermute(block, axis, route)  14.9 us
    pallas_call x1, Pallas kernels, gather_heads(): pl.pallas_call(gather_kernel, out_shape=jax.ShapeDtypeStruct((mixed.shape...  13.1 us
    ppermute x5, waiting for transfers between devices, passed_along(): return lax.ppermute(block, axis, route)  11.6 us
    dot_general x1, matrix products, body(): jnp.dot(heads0.transpose(1, 0, 2).reshape(seq_len, tp_count * HEAD_DIM),...  8.75 us
    reduce_sum x1, other arithmetic, project(): jnp.mean(row_float * row_float, axis=1, keepdims=True) + NORM_EPS  5.47 us
    dot_general x3, matrix products, project(): jnp.dot(normed, w, preferred_element_type=jnp.float32).astype(jnp.bfloat16)  5.39 us
    dot_general x3, matrix products, body(): jnp.dot(geared, weights_half[j], preferred_element_type=jnp.float32)  5.18 us
  transfers between devices with their start and end apart: 7, of which 3 were waited for; matrix products, arithmetic and copies ran while one was open for 21% of the time, Pallas kernels for 56%

profile of v4, /device:TPU:0, one launch (start us, length us, event | category | flops | bytes accessed | tf_op | source)
XLA Modules:
  0.0 163.0 jit_solution(1312970440822570513)
XLA Ops:
  0.6 0.8 reduce.16
  1.5 3.0 %collective-permute-start.2 = (bf16[6144]{0:T(1024)(128)(2,1)S(1)}, bf16[6144]{0:T(1024)(128)(2,1)S(1)}, u32[]{:S(2)}, u32[]{:S(2)}) collective-permute-start(bf16[6144]{0:T(1024)(128)(2,1)S(1)} %reduce.16), channel_id=1, source_target_pairs={{8,0},{0,8},{9,1},{1,9},{10,2},{2,10},{11,3},{3,11},{12,4},{4,12},... | collective-permute-start | bytes 36872 | tf_op jit(solution)/shard_map/ppermute | solution.py:20
  4.5 0.8 add.108
  5.3 5.5 %fusion = (f32[512]{0:T(512)S(1)}, bf16[512,6144]{1,0:T(8,128)(2,1)S(1)}) fusion(f32[6144]{0:T(1024)S(1)} %bitcast.100, bf16[512,6144]{1,0:T(8,128)(2,1)} %param.11), kind=kLoop, calls=%fused_computation.2 | loop fusion | flops 18873856 | bytes 12609536 | tf_op jit(solution)/shard_map/reduce_sum | solution.py:432
  10.8 2.5 %fusion.2 = bf16[512,6144]{1,0:T(8,128)(2,1)S(1)} fusion(bf16[512,6144]{1,0:T(8,128)(2,1)S(1)} %get-tuple-element.16, f32[6144]{0:T(1024)S(1)} %mul.99, f32[512]{0:T(512)S(1)} %add_rsqrt_fusion.1), kind=kLoop, calls=%fused_computation.4 | loop fusion | flops 12582912 | bytes 12609536 | tf_op jit(solution)/shard_map/convert_element_type | solution.py:434
  13.5 1.8 %convolution_convert_fusion = bf16[512,128]{1,0:T(8,128)(2,1)S(1)} fusion(bf16[512,6144]{1,0:T(8,128)(2,1)S(1)} %fusion.2, bf16[1,6144,128]{2,1,0:T(8,128)(2,1)S(1)} %copy-done.3), kind=kOutput, calls=%fused_computation.28 | convolution fusion | flops 805371904 | bytes 7995392 | tf_op jit(solution)/shard_map/dot_general | solution.py:436
  15.3 1.8 %convolution_convert_fusion.1 = bf16[512,128]{1,0:T(8,128)(2,1)S(1)} fusion(bf16[512,6144]{1,0:T(8,128)(2,1)S(1)} %fusion.2, bf16[1,6144,128]{2,1,0:T(8,128)(2,1)S(1)} %copy-done.2), kind=kOutput, calls=%fused_computation.29 | convolution fusion | flops 805371904 | bytes 7995392 | tf_op jit(solution)/shard_map/dot_general | solution.py:436
  17.3 1.8 %convolution_convert_fusion.2 = bf16[512,128]{1,0:T(8,128)(2,1)S(1)} fusion(bf16[512,6144]{1,0:T(8,128)(2,1)S(1)} %fusion.2, bf16[1,6144,128]{2,1,0:T(8,128)(2,1)S(1)} %copy-done.4), kind=kOutput, calls=%fused_computation.30 | convolution fusion | flops 805371904 | bytes 7995392 | tf_op jit(solution)/shard_map/dot_general | solution.py:436
  19.5 0.4 fusion.61
  20.2 0.4 fusion.42
  20.6 1.0 fusion.19.mixed
  21.6 77.8 %shard_map.130 = (bf16[1024,3072]{1,0:T(8,128)(2,1)}, bf16[8,512,128]{2,1,0:T(8,128)(2,1)}, bf16[3,3072,128]{2,1,0:T(8,128)(2,1)}, bf16[2,1024,384]{2,1,0:T(8,128)(2,1)}) custom-call(bf16[128,6144]{1,0:T(8,128)(2,1)} %bitcast.94, bf16[6144,128]{1,0:T(8,128)(2,1)} %bitcast.95, bf16[6144,128]{1,0:T(8,128)(2,1)} %bitcast.96, bf16[6144,128]{1,0:T(8,128)(2,1)} %bitcast.97, ...), custom_call_target="tpu_custom_call" | custom-call | tf_op jit(solution)/shard_map/pallas_call | solution.py:316
  99.5 1.5 copy.26
  101.0 8.8 %fusion.4 = (f32[512]{0:T(512)S(1)}, bf16[512,3072]{1,0:T(8,128)(2,1)}) fusion(bf16[512,1024]{0,1:T(8,128)(2,1)S(1)} %bitcast.98, bf16[1024,3072]{1,0:T(8,128)(2,1)} %get-tuple-element.8, bf16[512,6144]{1,0:T(8,128)(2,1)} %copy-done.1, s32[]{:T(128)S(6)} %select_n.95), kind=kOutput, calls=%fused_computation.9 | convolution fusion | flops 3230662144 | bytes 13633540 | tf_op jit(solution)/shard_map/dot_general | solution.py:450
  109.7 3.2 %fusion.9 = f32[512,128]{1,0:T(8,128)S(1)} fusion(bf16[512,3072]{1,0:T(8,128)(2,1)} %get-tuple-element.24, f32[3072]{0:T(1024)S(1)} %fusion.56, bf16[3,3072,128]{2,1,0:T(8,128)(2,1)} %get-tuple-element.9), kind=kOutput, calls=%fused_computation.13 | convolution fusion | flops 407371776 | bytes 4206592 | tf_op jit(solution)/shard_map/dot_general | solution.py:460
  113.0 0.5 copy-done.6
  113.5 1.0 fusion.7
  114.5 1.0 fusion.5
  115.5 7.7 %collective-permute-start.3 = (bf16[512,384]{1,0:T(8,128)(2,1)S(1)}, bf16[512,384]{1,0:T(8,128)(2,1)S(1)}, u32[]{:S(2)}, u32[]{:S(2)}) collective-permute-start(bf16[512,384]{1,0:T(8,128)(2,1)S(1)} %fusion.41), channel_id=1, source_target_pairs={{8,0},{0,8},{9,1},{1,9},{10,2},{2,10},{11,3},{3,11},{12,4},{4,12},... | collective-permute-start | bytes 1179656 | tf_op jit(solution)/shard_map/ppermute | solution.py:20
  123.3 1.2 constant_dynamic-slice_fusion.1
  124.5 2.0 %collective-permute-start = (bf16[512,768]{1,0:T(8,128)(2,1)S(1)}, bf16[512,768]{1,0:T(8,128)(2,1)S(1)}, u32[]{:S(2)}, u32[]{:S(2)}) collective-permute-start(bf16[512,768]{1,0:T(8,128)(2,1)S(1)} %constant_dynamic-slice_fusion.1), channel_id=1, source_target_pairs={{8,0},{0,8},{9,1},{1,9},{10,2},{2,10},{11,3},{3,11},{12,4},{4,12},... | collective-permute-start | bytes 2359304 | tf_op jit(solution)/shard_map/ppermute | solution.py:20
  126.5 6.8 %collective-permute-done.4 = f32[512]{0:T(512)S(1)} collective-permute-done((f32[512]{0:T(512)S(1)}, f32[512]{0:T(512)S(1)}, u32[]{:S(2)}, u32[]{:S(2)}) %collective-permute-start.4) | collective-permute-done | bytes 2080 | tf_op jit(solution)/shard_map/ppermute | solution.py:20
  133.5 0.4 fusion.63
  135.4 1.2 collective-permute-done.5
  136.7 13.1 %shard_map.131 = bf16[256,1024]{1,0:T(8,128)(2,1)S(1)} custom-call(bf16[256,128]{1,0:T(8,128)(2,1)S(1)} %fusion.47.mixed), custom_call_target="tpu_custom_call" | custom-call | tf_op jit(solution)/shard_map/pallas_call | solution.py:376
  149.9 1.3 broadcast_select_fusion
  151.3 1.6 fusion.31
  152.9 1.6 fusion.29
  154.7 2.0 %collective-permute-start.6 = (bf16[128,768]{1,0:T(8,128)(2,1)S(1)}, bf16[128,768]{1,0:T(8,128)(2,1)S(1)}, u32[]{:S(2)}, u32[]{:S(2)}) collective-permute-start(bf16[128,768]{1,0:T(8,128)(2,1)S(1)} %slice.28), channel_id=1, source_target_pairs={{8,0},{0,8},{9,1},{1,9},{10,2},{2,10},{11,3},{3,11},{12,4},{4,12},... | collective-permute-start | bytes 589832 | tf_op jit(solution)/shard_map/ppermute | solution.py:20
  156.8 0.7 select_bitcast_fusion
  157.5 4.8 %collective-permute-done.6 = bf16[128,768]{1,0:T(8,128)(2,1)S(1)} collective-permute-done((bf16[128,768]{1,0:T(8,128)(2,1)S(1)}, bf16[128,768]{1,0:T(8,128)(2,1)S(1)}, u32[]{:S(2)}, u32[]{:S(2)}) %collective-permute-start.6) | collective-permute-done | bytes 196640 | tf_op jit(solution)/shard_map/ppermute | solution.py:20
  162.3 0.7 slice_select_fusion
  (53 shorter events, 3.2 us)
Async XLA Ops:
  0.6 18.8 %copy-start = (bf16[1,1,512,128]{3,2,1,0:T(8,128)(2,1)S(1)}, bf16[1,1,512,128]{3,2,1,0:T(8,128)(2,1)}, u32[]{:S(2)}) copy-start(bf16[1,1,512,128]{3,2,1,0:T(8,128)(2,1)} %param.18) | copy-start | bytes 393220
  1.5 108.2 %collective-permute-start.2 = (bf16[6144]{0:T(1024)(128)(2,1)S(1)}, bf16[6144]{0:T(1024)(128)(2,1)S(1)}, u32[]{:S(2)}, u32[]{:S(2)}) collective-permute-start(bf16[6144]{0:T(1024)(128)(2,1)S(1)} %reduce.16), channel_id=1, source_target_pairs={{8,0},{0,8},{9,1},{1,9},{10,2},{2,10},{11,3},{3,11},{12,4},{4,12},... | collective-permute-start | bytes 36872 | tf_op jit(solution)/shard_map/ppermute | solution.py:20
  10.8 2.7 %copy-start.1 = (bf16[512,6144]{1,0:T(8,128)(2,1)}, bf16[512,6144]{1,0:T(8,128)(2,1)S(1)}, u32[]{:S(2)}) copy-start(bf16[512,6144]{1,0:T(8,128)(2,1)S(1)} %get-tuple-element.16) | copy-start | bytes 18874372
  10.8 2.7 %copy-start.3 = (bf16[1,6144,128]{2,1,0:T(8,128)(2,1)S(1)}, bf16[1,6144,128]{2,1,0:T(8,128)(2,1)}, u32[]{:S(2)}) copy-start(bf16[1,6144,128]{2,1,0:T(8,128)(2,1)} %param.15) | copy-start | bytes 4718596
  13.4 1.8 %copy-start.2 = (bf16[1,6144,128]{2,1,0:T(8,128)(2,1)S(1)}, bf16[1,6144,128]{2,1,0:T(8,128)(2,1)}, u32[]{:S(2)}) copy-start(bf16[1,6144,128]{2,1,0:T(8,128)(2,1)} %param.14) | copy-start | bytes 4718596
  13.4 3.6 %copy-start.9 = (s32[4]{0:T(128)S(1)}, s32[4]{0:T(128)}, u32[]{:S(2)}) copy-start(s32[4]{0:T(128)} %param.20) | copy-start | bytes 52
  13.4 3.8 %copy-start.10 = (s32[4]{0:T(128)S(1)}, s32[4]{0:T(128)}, u32[]{:S(2)}) copy-start(s32[4]{0:T(128)} %param.21) | copy-start | bytes 52
  13.5 3.9 %copy-start.4 = (bf16[1,6144,128]{2,1,0:T(8,128)(2,1)S(1)}, bf16[1,6144,128]{2,1,0:T(8,128)(2,1)}, u32[]{:S(2)}) copy-start(bf16[1,6144,128]{2,1,0:T(8,128)(2,1)} %param.16) | copy-start | bytes 4718596
  19.1 1.5 copy-start.7
  109.7 3.3 %copy-start.5 = (bf16[512,3072]{1,0:T(8,128)(2,1)S(1)}, bf16[512,3072]{1,0:T(8,128)(2,1)}, u32[]{:S(2)}) copy-start(bf16[512,3072]{1,0:T(8,128)(2,1)} %get-tuple-element.24) | copy-start | bytes 9437188
  109.7 3.8 %copy-start.6 = (bf16[3,3072,128]{2,1,0:T(8,128)(2,1)S(1)}, bf16[3,3072,128]{2,1,0:T(8,128)(2,1)}, u32[]{:S(2)}) copy-start(bf16[3,3072,128]{2,1,0:T(8,128)(2,1)} %get-tuple-element.9) | copy-start | bytes 7077892
  115.5 17.8 %collective-permute-start.3 = (bf16[512,384]{1,0:T(8,128)(2,1)S(1)}, bf16[512,384]{1,0:T(8,128)(2,1)S(1)}, u32[]{:S(2)}, u32[]{:S(2)}) collective-permute-start(bf16[512,384]{1,0:T(8,128)(2,1)S(1)} %fusion.41), channel_id=1, source_target_pairs={{8,0},{0,8},{9,1},{1,9},{10,2},{2,10},{11,3},{3,11},{12,4},{4,12},... | collective-permute-start | bytes 1179656 | tf_op jit(solution)/shard_map/ppermute | solution.py:20
  123.3 10.1 %collective-permute-start.4 = (f32[512]{0:T(512)S(1)}, f32[512]{0:T(512)S(1)}, u32[]{:S(2)}, u32[]{:S(2)}) collective-permute-start(f32[512]{0:T(512)S(1)} %get-tuple-element.23), channel_id=1, source_target_pairs={{8,0},{0,8},{9,1},{1,9},{10,2},{2,10},{11,3},{3,11},{12,4},{4,12},... | collective-permute-start | bytes 6152 | tf_op jit(solution)/shard_map/ppermute | solution.py:20
  124.5 25.3 %collective-permute-start = (bf16[512,768]{1,0:T(8,128)(2,1)S(1)}, bf16[512,768]{1,0:T(8,128)(2,1)S(1)}, u32[]{:S(2)}, u32[]{:S(2)}) collective-permute-start(bf16[512,768]{1,0:T(8,128)(2,1)S(1)} %constant_dynamic-slice_fusion.1), channel_id=1, source_target_pairs={{8,0},{0,8},{9,1},{1,9},{10,2},{2,10},{11,3},{3,11},{12,4},{4,12},... | collective-permute-start | bytes 2359304 | tf_op jit(solution)/shard_map/ppermute | solution.py:20
  126.5 8.4 %copy-start.8 = (bf16[1,1,512,128]{3,2,1,0:T(8,128)(2,1)S(1)}, bf16[1,1,512,128]{3,2,1,0:T(8,128)(2,1)}, u32[]{:S(2)}) copy-start(bf16[1,1,512,128]{3,2,1,0:T(8,128)(2,1)} %param.19) | copy-start | bytes 393220
  135.4 1.3 collective-permute-start.5
  151.2 3.2 %collective-permute-start.1 = (bf16[256,768]{1,0:T(8,128)(2,1)S(1)}, bf16[256,768]{1,0:T(8,128)(2,1)S(1)}, u32[]{:S(2)}, u32[]{:S(2)}) collective-permute-start(bf16[256,768]{1,0:T(8,128)(2,1)S(1)} %constant_dynamic-slice_fusion), channel_id=1, source_target_pairs={{0,16},{16,0},{1,17},{17,1},{2,18},{18,2},{3,19},{19,3},{4,20},{20... | collective-permute-start | bytes 1179656 | tf_op jit(solution)/shard_map/ppermute | solution.py:24
  154.7 7.6 %collective-permute-start.6 = (bf16[128,768]{1,0:T(8,128)(2,1)S(1)}, bf16[128,768]{1,0:T(8,128)(2,1)S(1)}, u32[]{:S(2)}, u32[]{:S(2)}) collective-permute-start(bf16[128,768]{1,0:T(8,128)(2,1)S(1)} %slice.28), channel_id=1, source_target_pairs={{8,0},{0,8},{9,1},{1,9},{10,2},{2,10},{11,3},{3,11},{12,4},{4,12},... | collective-permute-start | bytes 589832 | tf_op jit(solution)/shard_map/ppermute | solution.py:20
